TPU v7x, 128 devices: a whole 4x4x4 slice. The times are simulated.
128 devices in a mesh: dp: 8 (over z_hi, x), mp: 16 (over z_lo, y, core).
Axes of the slice: x: 4, y: 4, z: 4 (z_hi: 2, z_lo: 2; z = z_hi * 2 + z_lo), core: 2. Of those that a mesh axis runs over, the one named last changes fastest.
Arguments:
- tokens: bfloat16 [6144, 8192], P('dp', 'mp'), may hold values from -6 to 6
- out_grad: bfloat16 [6144, 8192], P('dp', 'mp'), may hold values from -6 to 6
- first_blocks: bfloat16 [64, 5, 256, 256], P('mp'), may hold values from -0.15625 to 0.15625
- first_index: int32 [64, 5], P('mp'), may hold values from 0 to 1
- second_blocks: bfloat16 [32, 5, 256, 256], P('mp'), may hold values from -0.15625 to 0.15625
- second_index: int32 [32, 5], P('mp'), may hold values from 0 to 3
- first_left: bfloat16 [8192, 512], P('mp'), may hold values from -0.0625 to 0.0625
- first_right: bfloat16 [512, 16384], P(None, 'mp'), may hold values from -0.25 to 0.25
- second_left: bfloat16 [16384, 512], P('mp'), may hold values from -0.046875 to 0.046875
- second_right: bfloat16 [512, 8192], P(None, 'mp'), may hold values from -0.25 to 0.25
Outputs:
- output: bfloat16 [6144, 8192], P('dp', 'mp')
- tokens_grad: bfloat16 [6144, 8192], P('dp', 'mp')
- first_blocks_grad: bfloat16 [64, 5, 256, 256], P('mp')
- first_left_grad: bfloat16 [8192, 512], P('mp')
- first_right_grad: bfloat16 [512, 16384], P(None, 'mp')
- second_blocks_grad: bfloat16 [32, 5, 256, 256], P('mp')
- second_left_grad: bfloat16 [16384, 512], P('mp')
- second_right_grad: bfloat16 [512, 8192], P(None, 'mp')
All inputs are finite; a program needn't handle non-finite values.
Results may differ from a plain program's by a relative error of at most 0.015.
Values may be sent and summed in bfloat16 or wider, within the bound.
A program may use at most 128 MiB of HBM per device.

v0:
```python
import jax
import jax.numpy as jnp
from jax import lax
from jax.sharding import PartitionSpec as P


def partner(block, axis, distance):
    count = lax.axis_size(axis)
    route = []
    for low in range(count):
        high = low | 1 << distance
        if high != low and high < count:
            route += [(low, high), (high, low)]
    return lax.ppermute(block, axis, route)


def one_hot(index, count):
    return (index[..., None] == jnp.arange(count, dtype=jnp.int32)).astype(jnp.float32)


def rounded(values):
    return lax.optimization_barrier(values.astype(jnp.bfloat16)).astype(jnp.float32)


def inner(left, right):
    return lax.dot_general(
        left, right, (((0,), (0,)), ((), ())), preferred_element_type=jnp.float32
    )


def across(left, right):
    return lax.dot_general(
        left, right, (((1,), (1,)), ((), ())), preferred_element_type=jnp.float32
    )


def rank_total(partial_value):
    total = lax.psum(partial_value, "mp").astype(jnp.bfloat16)
    return total


def hidden_level(grads, weights, hot):
    flow = jnp.einsum("teo,ejo->tej", grads, weights, preferred_element_type=jnp.float32)
    return jnp.einsum("tej,ed->tdj", flow, hot)


def token_level(grads, weights, hot):
    flow = jnp.einsum("tfo,fio->tfi", grads, weights, preferred_element_type=jnp.float32)
    return jnp.einsum("tfi,fd->tdi", flow, hot)


def body(
    tokens,
    out_grad,
    first_blocks,
    first_index,
    second_blocks,
    second_index,
    first_left,
    first_right,
    second_left,
    second_right,
):
    levels = lax.axis_size("mp").bit_length() - 1
    tok_rows = tokens.shape[0]
    hidden_count = first_blocks.shape[0]
    model_count = second_blocks.shape[0]
    width = first_blocks.shape[2]
    token_blocks = tokens.reshape(tok_rows, model_count, width)
    token_pieces = [token_blocks]
    for level in range(levels):
        token_pieces.append(partner(token_blocks, "mp", level))
    token_all = jnp.stack(token_pieces, axis=1)
    first_hot = one_hot(first_index, model_count)
    token_pick = jnp.einsum(
        "tkdi,fkd->tfki",
        token_all,
        first_hot.astype(jnp.bfloat16),
        preferred_element_type=jnp.float32,
    ).astype(jnp.bfloat16)
    block_first = jnp.einsum(
        "tfki,fkio->tfo", token_pick, first_blocks, preferred_element_type=jnp.float32
    )
    rank_first = rank_total(jnp.dot(tokens, first_left, preferred_element_type=jnp.float32))
    pre = block_first.reshape(tok_rows, -1) + jnp.dot(
        rank_first, first_right, preferred_element_type=jnp.float32
    )
    hidden = jax.nn.silu(pre).astype(jnp.bfloat16)
    hidden_blocks = hidden.reshape(tok_rows, hidden_count, width)
    hidden_pieces = [hidden_blocks]
    for level in range(levels):
        hidden_pieces.append(partner(hidden_blocks, "mp", level))
    hidden_all = jnp.stack(hidden_pieces, axis=1)
    second_hot = one_hot(second_index, hidden_count)
    hidden_pick = jnp.einsum(
        "tkdj,ekd->tekj",
        hidden_all,
        second_hot.astype(jnp.bfloat16),
        preferred_element_type=jnp.float32,
    ).astype(jnp.bfloat16)
    block_second = jnp.einsum(
        "tekj,ekjo->teo", hidden_pick, second_blocks, preferred_element_type=jnp.float32
    )
    rank_second = rank_total(jnp.dot(hidden, second_left, preferred_element_type=jnp.float32))
    output = (
        block_second.reshape(tok_rows, -1)
        + jnp.dot(rank_second, second_right, preferred_element_type=jnp.float32)
    ).astype(jnp.bfloat16)
    grad_blocks = out_grad.reshape(tok_rows, model_count, width)
    back_second = rank_total(across(out_grad, second_right))
    second_block_term = jnp.einsum(
        "tekj,teo->ekjo", hidden_pick, grad_blocks, preferred_element_type=jnp.float32
    )
    second_left_term = inner(hidden, back_second)
    second_right_term = inner(rank_second, out_grad)
    second_sums = lax.psum((second_block_term, second_left_term, second_right_term), "dp")
    hidden_sum = rounded(hidden_level(grad_blocks, second_blocks[:, 0], second_hot[:, 0]))
    for level in range(levels):
        part = hidden_level(
            grad_blocks, second_blocks[:, level + 1], second_hot[:, level + 1]
        ).astype(jnp.bfloat16)
        hidden_sum = hidden_sum + partner(part, "mp", level).astype(jnp.float32)
    hidden_grad = hidden_sum.reshape(tok_rows, -1) + across(back_second, second_left)
    sigma = jax.nn.sigmoid(pre)
    pre_grad = (hidden_grad * sigma * (1.0 + pre * (1.0 - sigma))).astype(jnp.bfloat16)
    pre_blocks = pre_grad.reshape(tok_rows, hidden_count, width)
    back_first = rank_total(across(pre_grad, first_right))
    first_block_term = jnp.einsum(
        "tfki,tfo->fkio", token_pick, pre_blocks, preferred_element_type=jnp.float32
    )
    first_left_term = inner(tokens, back_first)
    first_right_term = inner(rank_first, pre_grad)
    first_sums = lax.psum((first_block_term, first_left_term, first_right_term), "dp")
    token_sum = rounded(token_level(pre_blocks, first_blocks[:, 0], first_hot[:, 0]))
    for level in range(levels):
        part = token_level(pre_blocks, first_blocks[:, level + 1], first_hot[:, level + 1]).astype(
            jnp.bfloat16
        )
        token_sum = token_sum + partner(part, "mp", level).astype(jnp.float32)
    tokens_grad = (token_sum.reshape(tok_rows, -1) + across(back_first, first_left)).astype(
        jnp.bfloat16
    )
    return (
        output,
        tokens_grad,
        first_sums[0].astype(jnp.bfloat16),
        first_sums[1].astype(jnp.bfloat16),
        first_sums[2].astype(jnp.bfloat16),
        second_sums[0].astype(jnp.bfloat16),
        second_sums[1].astype(jnp.bfloat16),
        second_sums[2].astype(jnp.bfloat16),
    )


def solution(mesh):
    placed = (
        P("dp", "mp"),
        P("dp", "mp"),
        P("mp", None, None, None),
        P("mp", None),
        P("mp", None, None, None),
        P("mp", None),
        P("mp", None),
        P(None, "mp"),
        P("mp", None),
        P(None, "mp"),
    )
    return jax.shard_map(
        body,
        mesh=mesh,
        in_specs=placed,
        out_specs=(
            P("dp", "mp"),
            P("dp", "mp"),
            P("mp", None, None, None),
            P("mp", None),
            P(None, "mp"),
            P("mp", None, None, None),
            P("mp", None),
            P(None, "mp"),
        ),
        check_vma=False,
    )
```

profile of v0, /device:TPU:0, one launch (start us, length us, event | category | flops | bytes accessed | tf_op | source)
XLA Modules:
  0.0 717.8 jit_solution(4753544150908119829)
XLA Ops:
  0.7 3.0 reshape.42
  3.7 1.7 collective-permute-start.1
  5.4 2.9 collective-permute-start.2
  8.3 1.9 collective-permute-start.3
  12.3 1.8 copy.48
  14.3 3.4 fusion.44
  18.9 2.2 fusion.110
  21.1 2.3 fusion.112
  23.3 2.2 fusion.116
  25.6 1.7 fusion.128
  27.3 1.8 fusion.131
  29.1 3.0 copy.47
  32.1 3.4 fusion.41
  35.5 1.8 copy.46
  37.2 3.4 fusion.38
  40.6 1.8 copy.44
  42.4 3.4 fusion.32
  45.8 69.5 %all-reduce.6 = (bf16[768,512]{1,0:T(8,128)(2,1)}, bf16[768,512]{1,0:T(8,128)(2,1)S(1)}) all-reduce(f32[768,512]{1,0:T(8,128)} %fusion.128, f32[768,512]{1,0:T(8,128)} %fusion.131), channel_id=1, replica_groups=mesh['dp'=8,'mp'=16] {'mp'}, use_global_device_ids=true, to_apply=%region_0.0 | all-reduce | flops 786432 | bytes 4718592 | tf_op jit(solution)/shard_map/psum | solution.py:38
  116.1 2.7 fusion.135
  118.8 1.4 fusion.114
  120.2 1.4 constant_dynamic-update-slice_fusion
  122.5 2.3 fusion.35
  124.9 2.6 bitcast_dynamic-update-slice_fusion.7
  127.5 2.6 bitcast_dynamic-update-slice_fusion.6
  130.7 2.6 bitcast_dynamic-update-slice_fusion.5
  133.3 2.6 bitcast_dynamic-update-slice_fusion.4
  135.8 8.1 %convert_bitcast_fusion = bf16[768,4,5,256]{3,1,0,2:T(4,128)(2,1)} fusion(bf16[768,5,2,256]{3,2,0,1:T(2,128)(2,1)} %bitcast_dynamic-update-slice_fusion.4, pred[4,5,2]{2,0,1:T(4,128)(4,1)S(1)} %iota_compare_fusion), kind=kOutput, calls=%fused_computation | convolution fusion | flops 19660880 | bytes 11796520 | tf_op jit(solution)/shard_map/tkdi,fkd->tfki/dot_general | solution.py:75
  143.9 13.1 %copy.32 = bf16[768,4,5,256]{0,3,2,1:T(8,128)(2,1)} copy(bf16[768,4,5,256]{3,1,0,2:T(4,128)(2,1)} %convert_bitcast_fusion) | data formatting | bytes 15728640 | tf_op jit(solution)/shard_map/convert_element_type | solution.py:80
  157.1 7.9 %fusion.127 = f32[4,768,256,1]{1,2,3,0:T(8,128)} fusion(bf16[768,4,5,256]{0,3,2,1:T(8,128)(2,1)} %copy.32, bf16[4,5,256,256]{3,2,1,0:T(8,128)(2,1)} %param.12), kind=kOutput, calls=%fused_computation.136 | convolution fusion | flops 2013265920 | bytes 13631488 | tf_op jit(solution)/shard_map/tfki,fkio->tfo/dot_general | solution.py:81
  165.0 3.6 copy.23
  168.6 3.5 convolution_add_fusion
  172.2 21.8 %collective-permute-done.9 = bf16[768,4,256]{2,1,0:T(4,128)(2,1)} collective-permute-done((bf16[768,4,256]{2,1,0:T(4,128)(2,1)}, bf16[768,4,256]{2,1,0:T(4,128)(2,1)}, u32[]{:S(2)}, u32[]{:S(2)}) %collective-permute-start.9) | collective-permute-done | bytes 1572896 | tf_op jit(solution)/shard_map/ppermute | solution.py:14
  194.0 3.3 convert_add_fusion
  199.1 2.9 multiply_convert_fusion
  202.1 2.6 reshape.44
  204.7 2.1 fusion.130
  206.8 2.3 fusion.132
  212.6 4.6 fusion.26
  217.2 2.3 fusion.137
  219.5 2.3 fusion.134
  221.9 2.4 fusion.62
  225.4 2.4 fusion.65
  228.9 2.4 fusion.68
  231.3 2.4 fusion.71
  233.7 89.1 %all-reduce.7 = (bf16[768,512]{1,0:T(8,128)(2,1)}, bf16[768,512]{1,0:T(8,128)(2,1)}) all-reduce(f32[768,512]{1,0:T(8,128)} %fusion.130, f32[768,512]{1,0:T(8,128)} %fusion.132), channel_id=1, replica_groups=mesh['dp'=8,'mp'=16] {'mp'}, use_global_device_ids=true, to_apply=%region_1.2 | all-reduce | flops 786432 | bytes 4718592 | tf_op jit(solution)/shard_map/psum | solution.py:38
  322.8 2.2 fusion.24
  325.0 1.6 convolution_bitcast_fusion
  326.6 1.6 fusion.136
  328.2 1.6 fusion.74
  329.8 2.4 stack_reshape.7
  332.2 2.1 constant_dynamic-update-slice_fusion.1
  336.6 2.3 convert_add_fusion.1
  340.2 2.0 bitcast_dynamic-update-slice_fusion.3
  342.2 23.6 %collective-permute-done.5 = bf16[768,4,256]{2,1,0:T(4,128)(2,1)} collective-permute-done((bf16[768,4,256]{2,1,0:T(4,128)(2,1)}, bf16[768,4,256]{2,1,0:T(4,128)(2,1)}, u32[]{:S(2)}, u32[]{:S(2)}) %collective-permute-start.5) | collective-permute-done | bytes 1572896 | tf_op jit(solution)/shard_map/ppermute | solution.py:14
  365.8 2.0 bitcast_dynamic-update-slice_fusion.2
  367.9 29.9 %collective-permute-done.6 = bf16[768,4,256]{2,1,0:T(4,128)(2,1)S(1)} collective-permute-done((bf16[768,4,256]{2,1,0:T(4,128)(2,1)}, bf16[768,4,256]{2,1,0:T(4,128)(2,1)S(1)}, u32[]{:S(2)}, u32[]{:S(2)}) %collective-permute-start.6) | collective-permute-done | bytes 1572896 | tf_op jit(solution)/shard_map/ppermute | solution.py:14
  399.1 6.1 fusion
  405.2 10.6 %copy.34 = bf16[768,2,5,256]{0,3,2,1:T(8,128)(2,1)} copy(bf16[768,2,5,256]{3,1,0,2:T(2,128)(2,1)} %fusion) | data formatting | bytes 7864320 | tf_op jit(solution)/shard_map/convert_element_type | solution.py:100
  415.8 4.5 fusion.129
  420.3 1.9 copy.26
  422.2 2.6 add_convert_fusion.1
  424.8 4.9 fusion.77
  429.7 285.9 %all-reduce.8 = (bf16[4,5,256,256]{3,2,1,0:T(8,128)(2,1)}, bf16[512,512]{0,1:T(8,128)(2,1)}, bf16[512,1024]{1,0:T(8,128)(2,1)}, bf16[2,5,256,256]{3,2,1,0:T(8,12...) all-reduce(f32[4,5,256,256]{3,2,1,0:T(8,128)} %fusion.26, ...), channel_id=1, replica_groups=mesh['dp'=8,'mp'=16] {'dp'}, use_global_device_ids=true, to_apply=%region_4.5 | all-reduce | flops 3538944 | bytes 21233664 | tf_op jit(solution)/shard_map/psum | solution.py:133
  715.6 2.0 copy.36
  (112 shorter events, 18.6 us)
Async XLA Ops:
  0.6 115.5 %copy-start = (bf16[1024,512]{1,0:T(8,128)(2,1)S(1)}, bf16[1024,512]{1,0:T(8,128)(2,1)}, u32[]{:S(2)}) copy-start(bf16[1024,512]{1,0:T(8,128)(2,1)} %param.18) | copy-start | bytes 3145732
  0.6 9.5 %copy-start.6 = (bf16[768,512]{1,0:T(8,128)(2,1)S(1)}, bf16[768,512]{1,0:T(8,128)(2,1)}, u32[]{:S(2)}) copy-start(bf16[768,512]{1,0:T(8,128)(2,1)} %param.11) | copy-start | bytes 2359300
  3.7 121.0 %collective-permute-start = (bf16[768,2,256]{2,1,0:T(2,128)(2,1)}, bf16[768,2,256]{2,1,0:T(2,128)(2,1)}, u32[]{:S(2)}, u32[]{:S(2)}) collective-permute-start(bf16[768,2,256]{2,1,0:T(2,128)(2,1)} %reshape.42), channel_id=1, source_target_pairs={{0,1},{1,0},{2,3},{3,2},{4,5},{5,4},{6,7},{7,6},{8,9},{9,8},{10,11... | collective-permute-start | bytes 2359304 | tf_op jit(solution)/shard_map/ppermute | solution.py:14
  3.7 123.8 %collective-permute-start.1 = (bf16[768,2,256]{2,1,0:T(2,128)(2,1)}, bf16[768,2,256]{2,1,0:T(2,128)(2,1)}, u32[]{:S(2)}, u32[]{:S(2)}) collective-permute-start(bf16[768,2,256]{2,1,0:T(2,128)(2,1)} %reshape.42), channel_id=1, source_target_pairs={{0,2},{2,0},{1,3},{3,1},{4,6},{6,4},{5,7},{7,5},{8,10},{10,8},{9,1... | collective-permute-start | bytes 2359304 | tf_op jit(solution)/shard_map/ppermute | solution.py:14
  5.4 124.7 %collective-permute-start.2 = (bf16[768,2,256]{2,1,0:T(2,128)(2,1)}, bf16[768,2,256]{2,1,0:T(2,128)(2,1)}, u32[]{:S(2)}, u32[]{:S(2)}) collective-permute-start(bf16[768,2,256]{2,1,0:T(2,128)(2,1)} %reshape.42), channel_id=1, source_target_pairs={{0,4},{4,0},{1,5},{5,1},{2,6},{6,2},{3,7},{7,3},{8,12},{12,8},{9,1... | collective-permute-start | bytes 2359304 | tf_op jit(solution)/shard_map/ppermute | solution.py:14
  8.3 125.0 %collective-permute-start.3 = (bf16[768,2,256]{2,1,0:T(2,128)(2,1)}, bf16[768,2,256]{2,1,0:T(2,128)(2,1)}, u32[]{:S(2)}, u32[]{:S(2)}) collective-permute-start(bf16[768,2,256]{2,1,0:T(2,128)(2,1)} %reshape.42), channel_id=1, source_target_pairs={{0,8},{8,0},{1,9},{9,1},{2,10},{10,2},{3,11},{11,3},{4,12},{12,4},... | collective-permute-start | bytes 2359304 | tf_op jit(solution)/shard_map/ppermute | solution.py:14
  10.4 1.9 copy-start.4
  11.0 3.2 copy-start.30
  14.1 3.7 copy-start.3
  17.7 154.5 %collective-permute-start.11 = (bf16[768,4,256]{2,1,0:T(4,128)(2,1)}, bf16[768,4,256]{2,1,0:T(4,128)(2,1)}, u32[]{:S(2)}, u32[]{:S(2)}) collective-permute-start(bf16[768,4,256]{2,1,0:T(4,128)(2,1)} %fusion.44), channel_id=1, source_target_pairs={{0,8},{8,0},{1,9},{9,1},{2,10},{10,2},{3,11},{11,3},{4,12},{12,4},... | collective-permute-start | bytes 4718600 | tf_op jit(solution)/shard_map/ppermute | solution.py:14
  21.1 4.5 copy-start.22
  25.6 1.7 copy-start.7
  25.6 1.7 copy-start.21
  32.1 3.4 copy-start.14
  37.2 3.4 copy-start.13
  115.3 0.9 copy-start.26
  118.8 1.4 copy-start.17
  118.8 2.8 copy-start.29
  124.8 47.4 %collective-permute-start.10 = (bf16[768,4,256]{2,1,0:T(4,128)(2,1)}, bf16[768,4,256]{2,1,0:T(4,128)(2,1)S(1)}, u32[]{:S(2)}, u32[]{:S(2)}) collective-permute-start(bf16[768,4,256]{2,1,0:T(4,128)(2,1)} %fusion.41), channel_id=1, source_target_pairs={{0,4},{4,0},{1,5},{5,1},{2,6},{6,2},{3,7},{7,3},{8,12},{12,8},{9,1... | collective-permute-start | bytes 4718600 | tf_op jit(solution)/shard_map/ppermute | solution.py:14
  127.5 66.5 %collective-permute-start.9 = (bf16[768,4,256]{2,1,0:T(4,128)(2,1)}, bf16[768,4,256]{2,1,0:T(4,128)(2,1)}, u32[]{:S(2)}, u32[]{:S(2)}) collective-permute-start(bf16[768,4,256]{2,1,0:T(4,128)(2,1)} %fusion.38), channel_id=1, source_target_pairs={{0,2},{2,0},{1,3},{3,1},{4,6},{6,4},{5,7},{7,5},{8,10},{10,8},{9,1... | collective-permute-start | bytes 4718600 | tf_op jit(solution)/shard_map/ppermute | solution.py:14
  130.1 63.9 %collective-permute-start.8 = (bf16[768,4,256]{2,1,0:T(4,128)(2,1)}, bf16[768,4,256]{2,1,0:T(4,128)(2,1)}, u32[]{:S(2)}, u32[]{:S(2)}) collective-permute-start(bf16[768,4,256]{2,1,0:T(4,128)(2,1)} %fusion.35), channel_id=1, source_target_pairs={{0,1},{1,0},{2,3},{3,2},{4,5},{5,4},{6,7},{7,6},{8,9},{9,8},{10,11... | collective-permute-start | bytes 4718600 | tf_op jit(solution)/shard_map/ppermute | solution.py:14
  168.6 25.4 %copy-start.24 = (bf16[768,4,256]{2,1,0:T(4,128)(2,1)S(1)}, bf16[768,4,256]{2,1,0:T(4,128)(2,1)}, u32[]{:S(2)}) copy-start(bf16[768,4,256]{2,1,0:T(4,128)(2,1)} %fusion.32) | copy-start | bytes 4718596
  197.3 1.9 copy-start.2
  204.7 2.1 copy-start.9
  204.7 2.1 copy-start.25
  206.8 2.3 copy-start.20
  209.1 2.5 slice-start
  210.3 2.3 slice-start.1
  212.6 4.6 copy-start.28
  217.2 2.3 copy-start.27
  221.8 118.4 %collective-permute-start.4 = (bf16[768,4,256]{2,1,0:T(4,128)(2,1)}, bf16[768,4,256]{2,1,0:T(4,128)(2,1)}, u32[]{:S(2)}, u32[]{:S(2)}) collective-permute-start(bf16[768,4,256]{2,1,0:T(4,128)(2,1)} %reshape.44), channel_id=1, source_target_pairs={{0,1},{1,0},{2,3},{3,2},{4,5},{5,4},{6,7},{7,6},{8,9},{9,8},{10,11... | collective-permute-start | bytes 4718600 | tf_op jit(solution)/shard_map/ppermute | solution.py:14
  224.3 103.9 %collective-permute-start.15 = (bf16[768,2,256]{2,1,0:T(2,128)(2,1)}, bf16[768,2,256]{2,1,0:T(2,128)(2,1)}, u32[]{:S(2)}, u32[]{:S(2)}) collective-permute-start(bf16[768,2,256]{2,1,0:T(2,128)(2,1)} %fusion.62), channel_id=1, source_target_pairs={{0,8},{8,0},{1,9},{9,1},{2,10},{10,2},{3,11},{11,3},{4,12},{12,4},... | collective-permute-start | bytes 2359304 | tf_op jit(solution)/shard_map/ppermute | solution.py:14
  227.8 106.5 %collective-permute-start.14 = (bf16[768,2,256]{2,1,0:T(2,128)(2,1)}, bf16[768,2,256]{2,1,0:T(2,128)(2,1)}, u32[]{:S(2)}, u32[]{:S(2)}) collective-permute-start(bf16[768,2,256]{2,1,0:T(2,128)(2,1)} %fusion.65), channel_id=1, source_target_pairs={{0,4},{4,0},{1,5},{5,1},{2,6},{6,2},{3,7},{7,3},{8,12},{12,8},{9,1... | collective-permute-start | bytes 2359304 | tf_op jit(solution)/shard_map/ppermute | solution.py:14
  231.3 104.2 %collective-permute-start.13 = (bf16[768,2,256]{2,1,0:T(2,128)(2,1)}, bf16[768,2,256]{2,1,0:T(2,128)(2,1)}, u32[]{:S(2)}, u32[]{:S(2)}) collective-permute-start(bf16[768,2,256]{2,1,0:T(2,128)(2,1)} %fusion.68), channel_id=1, source_target_pairs={{0,2},{2,0},{1,3},{3,1},{4,6},{6,4},{5,7},{7,5},{8,10},{10,8},{9,1... | collective-permute-start | bytes 2359304 | tf_op jit(solution)/shard_map/ppermute | solution.py:14
  233.7 102.8 %collective-permute-start.12 = (bf16[768,2,256]{2,1,0:T(2,128)(2,1)}, bf16[768,2,256]{2,1,0:T(2,128)(2,1)}, u32[]{:S(2)}, u32[]{:S(2)}) collective-permute-start(bf16[768,2,256]{2,1,0:T(2,128)(2,1)} %fusion.71), channel_id=1, source_target_pairs={{0,1},{1,0},{2,3},{3,2},{4,5},{5,4},{6,7},{7,6},{8,9},{9,8},{10,11... | collective-permute-start | bytes 2359304 | tf_op jit(solution)/shard_map/ppermute | solution.py:14
  322.8 2.2 copy-start.18
  325.0 1.6 copy-start.8
  325.0 1.6 copy-start.15
  328.2 37.6 %collective-permute-start.5 = (bf16[768,4,256]{2,1,0:T(4,128)(2,1)}, bf16[768,4,256]{2,1,0:T(4,128)(2,1)}, u32[]{:S(2)}, u32[]{:S(2)}) collective-permute-start(bf16[768,4,256]{2,1,0:T(4,128)(2,1)} %reshape.44), channel_id=1, source_target_pairs={{0,2},{2,0},{1,3},{3,1},{4,6},{6,4},{5,7},{7,5},{8,10},{10,8},{9,1... | collective-permute-start | bytes 4718600 | tf_op jit(solution)/shard_map/ppermute | solution.py:14
  332.2 2.7 copy-start.19
  332.2 2.7 copy-start.23
  334.3 63.5 %collective-permute-start.6 = (bf16[768,4,256]{2,1,0:T(4,128)(2,1)}, bf16[768,4,256]{2,1,0:T(4,128)(2,1)S(1)}, u32[]{:S(2)}, u32[]{:S(2)}) collective-permute-start(bf16[768,4,256]{2,1,0:T(4,128)(2,1)} %reshape.44), channel_id=1, source_target_pairs={{0,4},{4,0},{1,5},{5,1},{2,6},{6,2},{3,7},{7,3},{8,12},{12,8},{9,1... | collective-permute-start | bytes 4718600 | tf_op jit(solution)/shard_map/ppermute | solution.py:14
  335.5 62.9 %collective-permute-start.7 = (bf16[768,4,256]{2,1,0:T(4,128)(2,1)}, bf16[768,4,256]{2,1,0:T(4,128)(2,1)S(1)}, u32[]{:S(2)}, u32[]{:S(2)}) collective-permute-start(bf16[768,4,256]{2,1,0:T(4,128)(2,1)} %reshape.44), channel_id=1, source_target_pairs={{0,8},{8,0},{1,9},{9,1},{2,10},{10,2},{3,11},{11,3},{4,12},{12,4},... | collective-permute-start | bytes 4718600 | tf_op jit(solution)/shard_map/ppermute | solution.py:14
  405.2 10.6 %copy-start.10 = (bf16[2,5,256,256]{3,2,1,0:T(8,128)(2,1)S(1)}, bf16[2,5,256,256]{3,2,1,0:T(8,128)(2,1)}, u32[]{:S(2)}) copy-start(bf16[2,5,256,256]{3,2,1,0:T(8,128)(2,1)} %param.14) | copy-start | bytes 3932164
  420.3 2.0 copy-start.16
  422.2 2.6 copy-start.5
  424.8 4.9 copy-start.11
  424.8 4.9 copy-start.12
  429.7 287.9 %copy-start.1 = (bf16[1024,512]{1,0:T(8,128)(2,1)S(1)}, bf16[1024,512]{1,0:T(8,128)(2,1)}, u32[]{:S(2)}) copy-start(bf16[1024,512]{1,0:T(8,128)(2,1)} %param.18) | copy-start | bytes 3145732
where the time goes:
time: 728 us; the launch traced here: 718 us
  blocking collectives  444 us (61%)
  matrix products  102 us (14%)
  waiting for transfers between devices  75.4 us (10%)
  local copies, waits for them, and re-layouts  73.5 us (10%)
  starting transfers between devices  11.3 us (2%)
  other arithmetic  9.83 us (1%)
    psum x1, blocking collectives, body(): lax.psum((first_block_term, first_left_term, first_right_term), 'dp')  286 us
    psum x2, blocking collectives, rank_total(): total = lax.psum(partial_value, 'mp').astype(jnp.bfloat16)  159 us
    ppermute x16, waiting for transfers between devices, partner(): return lax.ppermute(block, axis, route)  75.4 us
    unnamed x79, local copies, waits for them, and re-layouts  22.2 us
    dot_general x5, matrix products, hidden_level(): return jnp.einsum('tej,ed->tdj', flow, hot)  15.8 us
  transfers between devices with their start and end apart: 16, of which 3 were waited for; matrix products, arithmetic and copies ran while one was open for 17% of the time, Pallas kernels for 0%

commit v1 on v0

v1 whole, which is shorter than its diff:
```python
import jax
import jax.numpy as jnp
from jax import lax
from jax.experimental import pallas as pl
from jax.experimental.pallas import tpu as pltpu
from jax.sharding import PartitionSpec as P

BF = jnp.bfloat16
F32 = jnp.float32
CHUNKS = 4


def nn(left, right):
    return jnp.dot(left, right, preferred_element_type=F32)


def nt(left, right):
    return lax.dot_general(left, right, (((1,), (1,)), ((), ())), preferred_element_type=F32)


def flip(bit, by):
    return 1 - bit if by else bit


def tile_of(index, at):
    hot = (index == at).astype(F32)
    return jnp.broadcast_to(hot, (16, 128)).astype(BF)


def masked(weights, tiles):
    parts = []
    for weight, tile in zip(weights, tiles):
        wide = jnp.concatenate([tile, tile], axis=1)
        tall = weight.reshape(weight.shape[0] // 16, 16, weight.shape[1])
        parts.append((tall * wide[None]).reshape(weight.shape))
    return jnp.concatenate(parts, axis=1)


class Place:
    def __init__(self):
        self.dp = lax.axis_index("dp")
        self.mp = lax.axis_index("mp")
        self.core = lax.rem(self.mp, 2)
        chip = lax.div(self.mp, 2)
        self.chip = chip
        self.y0 = lax.rem(chip, 2)
        self.y1 = lax.rem(lax.div(chip, 2), 2)
        self.z = lax.div(chip, 4)
        self.x0 = lax.rem(self.dp, 2)
        self.x1 = lax.rem(lax.div(self.dp, 2), 2)
        self.z_hi = lax.div(self.dp, 4)

    def mp_peer(self, chip_bits, core_bit=0):
        y0 = flip(self.y0, chip_bits & 1)
        y1 = flip(self.y1, chip_bits & 2)
        z = flip(self.z, chip_bits & 4)
        return (self.dp, ((z * 2 + y1) * 2 + y0) * 2 + flip(self.core, core_bit))

    def chip_peer(self, chip_bits):
        y0 = flip(self.y0, chip_bits & 1)
        y1 = flip(self.y1, chip_bits & 2)
        z = flip(self.z, chip_bits & 4)
        return (z * 2 + y1) * 2 + y0

    def dp_peer(self, bits):
        x0 = flip(self.x0, bits & 1)
        x1 = flip(self.x1, bits & 2)
        z = flip(self.z_hi, bits & 4)
        return ((z * 2 + x1) * 2 + x0, self.mp)

    def level(self, level):
        return [None, self.mp_peer(0, 1), self.mp_peer(1), self.mp_peer(2), self.mp_peer(4)][level]


def greet(peers):
    barrier = pltpu.get_barrier_semaphore()
    for peer in peers:
        pl.semaphore_signal(barrier, inc=1, device_id=peer, device_id_type=pl.DeviceIdType.MESH)
    pl.semaphore_wait(barrier, len(peers))


def remote(src, dst, sems, at, peer):
    send, recv = sems
    return pltpu.make_async_remote_copy(
        src_ref=src,
        dst_ref=dst,
        send_sem=send.at[at],
        recv_sem=recv.at[at],
        device_id=peer,
        device_id_type=pl.DeviceIdType.MESH,
    )


class RankSum:
    def __init__(self, place, rows, half, result, own, away, near, chip_sum, far, sems):
        self.place, self.result, self.sems = place, result, sems
        self.own, self.away, self.near, self.chip_sum, self.far = own, away, near, chip_sum, far
        self.part = rows // 8
        self.half = half
        self.columns = pl.ds(pl.multiple_of(place.core * half, half), half)
        self.rows = pl.ds(pl.multiple_of(place.chip * self.part, self.part), self.part)
        sibling = place.mp_peer(0, 1)
        self.cores = remote(away, near, sems, 0, sibling)
        self.scatter = []
        self.gather = []
        for bits in range(1, 8):
            other = pl.ds(pl.multiple_of(place.chip_peer(bits) * self.part, self.part), self.part)
            peer = place.mp_peer(bits)
            self.scatter.append(
                remote(chip_sum.at[:, other, :], far.at[bits - 1], sems, bits, peer)
            )
            mine = result.at[:, self.rows, self.columns]
            self.gather.append(remote(mine, mine, sems, 7 + bits, peer))
        whole = result.at[:, :, self.columns]
        self.back = remote(whole, whole, sems, 15, sibling)

    def set(self, which, own, away):
        self.own[which] = own
        self.away[which] = away.astype(BF)

    def start(self):
        self.cores.start()

    def step_chip(self):
        self.cores.wait()
        for which in range(2):
            self.chip_sum[which] = (self.own[which] + self.near[which].astype(F32)).astype(BF)
        for copy in self.scatter:
            copy.start()

    def step_sum(self):
        total = self.chip_sum[:, self.rows, :].astype(F32)
        for copy in self.scatter:
            copy.wait()
        for bits in range(7):
            total = total + self.far[bits].astype(F32)
        self.result[:, self.rows, self.columns] = total.astype(BF)
        for copy in self.gather:
            copy.start()

    def step_back(self):
        for copy in self.gather:
            copy.wait()
        self.back.start()

    def finish(self):
        self.back.wait()


class Spread:
    def __init__(self, place, src, dst, sems):
        blocked = len(src.shape) == 3
        blocks = src.shape[0] if blocked else 1
        rows = src.shape[-2]
        step = rows * blocks // CHUNKS

        def source(part, block):
            return src.at[block, part, :] if blocked else src.at[part, :]

        def target(slot, part, block):
            return dst.at[slot, block, part, :] if blocked else dst.at[slot, part, :]

        self.direct = [
            remote(src, dst.at[slot], sems, at, place.level(level))
            for at, (slot, level) in enumerate(((3, 4), (0, 1)))
        ]
        self.near = []
        self.onward = []
        at = 2
        for block in range(blocks):
            for start in range(0, rows, step):
                part = pl.ds(start, step)
                self.near.append(
                    remote(source(part, block), target(1, part, block), sems, at, place.level(2))
                )
                self.onward.append(
                    remote(
                        target(1, part, block),
                        target(2, part, block),
                        sems,
                        at + CHUNKS,
                        place.mp_peer(3),
                    )
                )
                at = at + 1

    def start_direct(self):
        for copy in self.direct:
            copy.start()

    def start_near(self, chunk):
        self.near[chunk].start()

    def pass_on(self, chunk):
        self.near[chunk].wait_recv()
        self.onward[chunk].start()

    def wait_direct(self):
        for copy in self.direct:
            copy.wait_recv()

    def wait_onward(self):
        for copy in self.onward:
            copy.wait_recv()

    def close(self):
        for copy in self.direct + self.near + self.onward:
            copy.wait_send()


class Reduced:
    def __init__(self, place, grad, lead, first, second, third, sems, credit, at):
        self.credit, self.at, self.lead = credit, at, lead
        blocks = pl.ds(lead, first.shape[1])
        self.grad, self.bufs = grad, (first, second, third)
        rows = grad.shape[2]
        x0, x1, z = place.x0, place.x1, place.z_hi
        cross = x0 + x1 - 2 * x0 * x1
        near, back, far = place.dp_peer(1), place.dp_peer(3), place.dp_peer(4)
        self.greeted = (near, back, far)
        self.steps = [[] for _ in range(6)]
        self.kept = [[] for _ in range(3)]
        for h in range(2):
            keys = (cross, x1, z) if h == 0 else (x1, x0, z)
            peers = (near, back, far) if h == 0 else (back, near, far)
            offset, size = 0, rows
            for step in range(3):
                size = size // 2
                keep = pl.ds(pl.multiple_of(offset + keys[step] * size, size), size)
                send = pl.ds(pl.multiple_of(offset + (1 - keys[step]) * size, size), size)
                self.kept[step].append(keep)
                self.steps[step].append(
                    remote(
                        grad.at[h, blocks, send, :],
                        self.bufs[step].at[h],
                        sems,
                        (at, h, step),
                        peers[step],
                    )
                )
                own = grad.at[h, blocks, keep, :]
                self.steps[5 - step].append(
                    remote(own, own, sems, (at, h, 5 - step), peers[step])
                )
                offset = offset + keys[step] * size

    def free(self, kind, peer):
        pl.semaphore_signal(
            self.credit.at[self.at, kind],
            inc=1,
            device_id=peer,
            device_id_type=pl.DeviceIdType.MESH,
        )

    def start(self, step):
        if step == 3:
            pl.semaphore_wait(self.credit.at[self.at, 1], 1)
        if step == 4:
            pl.semaphore_wait(self.credit.at[self.at, 0], 2)
        for copy in self.steps[step]:
            copy.start()

    def turn(self, step):
        self.wait(step)
        self.start(step + 1)

    def wait(self, step):
        for h, copy in enumerate(self.steps[step]):
            copy.wait()
            if step < 3:
                keep = self.kept[step][h]
                for n in range(self.bufs[step].shape[1]):
                    self.grad[h, self.lead + n, keep, :] = (
                        self.grad[h, self.lead + n, keep, :].astype(F32)
                        + self.bufs[step][h, n].astype(F32)
                    ).astype(BF)
        if step == 1:
            self.free(0, self.greeted[0])
            self.free(0, self.greeted[1])
        if step == 2:
            self.free(1, self.greeted[2])


def layer_kernel(
    tokens,
    out_grad,
    w1,
    index1,
    index1_rows,
    w2,
    index2,
    index2_sent,
    first_left,
    first_right,
    second_left,
    second_right,
    output,
    tokens_grad,
    g_w1,
    g_fl,
    g_fr,
    g_w2,
    g_sl,
    g_sr,
    tokens_own,
    tokens_in,
    grads_in,
    w2_in,
    index_in,
    index_smem,
    hidden,
    hidden_t,
    pre_grad,
    tokens_t,
    rank_first_t,
    slope,
    own,
    away,
    chip_sum,
    near_a,
    far_a,
    ranks_a,
    near_b,
    far_b,
    ranks_b,
    swap,
    sent,
    out_in,
    *rest,
):
    bufs, rest = rest[:21], rest[21:]
    (
        tok_send,
        tok_recv,
        grad_send,
        grad_recv,
        rank_send_a,
        rank_recv_a,
        rank_send_b,
        rank_recv_b,
        w_send,
        w_recv,
        i_send,
        i_recv,
        dp_send,
        dp_recv,
        credit,
        swap_send,
        swap_recv,
        x_send,
        x_recv,
        inbox_free,
        local,
    ) = rest
    place = Place()
    rows = pre_grad.shape[0]
    half = first_left.shape[1] // 2
    width = w1.shape[2]
    mine = pl.ds(pl.multiple_of(place.core * half, half), half)
    other = pl.ds(pl.multiple_of((1 - place.core) * half, half), half)

    loads = [
        pltpu.make_async_copy(
            tokens.at[:, pl.ds(d * width, width)], tokens_own.at[d], local.at[d]
        )
        for d in range(2)
    ]
    for load in loads:
        load.start()
    greet(
        [place.mp_peer(bits) for bits in range(1, 8)]
        + [place.mp_peer(0, 1)]
        + [place.dp_peer(bits) for bits in (1, 3, 4)]
    )
    spread_tok = Spread(place, tokens_own, tokens_in, (tok_send, tok_recv))
    spread_grad = Spread(place, out_grad, grads_in, (grad_send, grad_recv))
    sums_a = RankSum(
        place, rows, half, ranks_a, own, away, near_a, chip_sum, far_a, (rank_send_a, rank_recv_a)
    )
    sums_b = RankSum(
        place, rows, half, ranks_b, own, away, near_b, chip_sum, far_b, (rank_send_b, rank_recv_b)
    )
    w_copies = [
        remote(w2.at[:, level], w2_in.at[level - 1], (w_send, w_recv), level - 1, place.level(level))
        for level in (4, 2, 3, 1)
    ]
    i_copies = [
        remote(
            index2_sent.at[level],
            index_in.at[level - 1],
            (i_send, i_recv),
            level - 1,
            place.level(level),
        )
        for level in range(1, 5)
    ]
    dp_sems = (dp_send, dp_recv)
    grads = ((g_w2, 0), (g_sl, 0), (g_w1, 0), (g_w1, 5), (g_fr, 0), (g_sr, 0), (g_fl, 0))
    r_w2, r_sl, r_w1a, r_w1b, r_fr, r_sr, r_fl = [
        Reduced(place, grad, lead, *bufs[3 * at : 3 * at + 3], dp_sems, credit, at)
        for at, (grad, lead) in enumerate(grads)
    ]

    for load in loads:
        load.wait()
    for chunk in range(CHUNKS):
        spread_tok.start_near(chunk)
    spread_tok.start_direct()
    for copy in i_copies:
        copy.start()
    both = jnp.concatenate([tokens_own[0], tokens_own[1]], axis=1)
    sums_a.set(0, nn(both, first_left[:, mine]), nn(both, first_left[:, other]))
    sums_a.set(1, nt(out_grad[...], second_right[mine, :]), nt(out_grad[...], second_right[other, :]))
    sums_a.start()
    for d in range(2):
        tokens_t[0, d] = tokens_own[d].T
    spread_tok.pass_on(0)
    sums_a.step_chip()
    spread_grad.start_near(0)
    spread_grad.start_near(1)
    spread_tok.pass_on(1)
    spread_grad.start_direct()
    spread_tok.pass_on(2)
    spread_grad.start_near(2)
    spread_grad.start_near(3)
    spread_tok.pass_on(3)
    for copy in w_copies:
        copy.start()
    sums_a.step_sum()
    spread_tok.wait_direct()
    for level in (1, 4):
        for d in range(2):
            tokens_t[level, d] = tokens_in[level - 1, d].T
    sums_a.step_back()
    for d in range(2):
        tokens_t[2, d] = tokens_in[1, d].T
    spread_grad.pass_on(0)
    spread_tok.wait_onward()
    for d in range(2):
        tokens_t[3, d] = tokens_in[2, d].T
    sums_a.finish()
    rank_first_t[...] = ranks_a[0].T

    for f in range(4):
        columns = pl.ds(f * width, width)
        picks = []
        for level in range(5):
            at = index1[f, level]
            picks.append(tokens_own[at] if level == 0 else tokens_in[level - 1, at])
        pre = nn(jnp.concatenate(picks, axis=1), w1[f].reshape(5 * width, width))
        pre = pre + nn(ranks_a[0], first_right[:, columns])
        sigma = 1.0 / (1.0 + jnp.exp(-pre))
        active = (pre * sigma).astype(BF)
        hidden[f] = active
        hidden_t[f] = active.T
        slope[f] = sigma * (1.0 + pre * (1.0 - sigma))
        if f < 3:
            spread_grad.pass_on(f + 1)
    spread_tok.close()
    for peer in (place.level(1), place.level(2), place.mp_peer(3), place.level(4)):
        pl.semaphore_signal(inbox_free, inc=1, device_id=peer, device_id_type=pl.DeviceIdType.MESH)

    for copy in i_copies + w_copies:
        copy.wait()
    fetch = pltpu.make_async_copy(index_in, index_smem, local.at[0])
    fetch.start()
    fetch.wait()
    spread_grad.wait_direct()

    def index_of(level, e):
        return index2[e, 0] if level == 0 else index_smem[level - 1, 0, e]

    def weight_of(level, e):
        return w2[e, 0] if level == 0 else w2_in[level - 1, e]

    def second_grads(level):
        for e in range(2):
            columns = pl.ds(e * width, width)
            flow = out_grad[:, columns] if level == 0 else grads_in[level - 1, :, columns]
            g_w2[e, level] = nn(hidden_t[index_of(level, e)], flow).astype(BF)

    for d in range(4):
        part = pl.ds(d % 2 * width, width)
        g_sl[d // 2, 0, part, :] = nn(hidden_t[d], ranks_a[1]).astype(BF)
    r_sl.start(0)
    for level in (0, 1, 4, 2):
        second_grads(level)
    spread_grad.wait_onward()
    second_grads(3)
    r_w2.start(0)

    for d in range(4):
        columns = pl.ds(d * width, width)
        total = nt(ranks_a[1], second_left[columns, :])
        for level in range(5):
            weights = [weight_of(level, e) for e in range(2)]
            row = index2_sent if level == 0 else index_in
            at = max(level - 1, 0)
            tiles = [tile_of(row[at, 0:1, e : e + 1], d) for e in range(2)]
            flow = out_grad[...] if level == 0 else grads_in[level - 1]
            total = total + nt(flow, masked(weights, tiles))
        pre_grad[:, columns] = (total * slope[d]).astype(BF)
    spread_grad.close()
    r_sl.turn(0)
    r_w2.turn(0)

    units = jnp.concatenate([hidden[d] for d in range(4)], axis=1)
    sums_b.set(0, nn(units, second_left[:, mine]), nn(units, second_left[:, other]))
    sums_b.set(1, nt(pre_grad[...], first_right[mine, :]), nt(pre_grad[...], first_right[other, :]))
    sums_b.start()

    def first_grads(f):
        for level in range(5):
            g_w1[f // 2, (f % 2) * 5 + level] = nn(
                tokens_t[level, index1[f, level]], pre_grad[:, f * width : f * width + width]
            ).astype(BF)

    first_grads(0)
    first_grads(2)
    r_w1a.start(0)
    sums_b.step_chip()
    first_grads(1)
    first_grads(3)
    r_w1b.start(0)
    for h in range(2):
        g_fr[h, 0] = nn(rank_first_t[h * 256 : h * 256 + 256, :], pre_grad[...]).astype(BF)
    r_fr.start(0)
    r_sl.turn(1)
    r_w2.turn(1)

    def out_part(level, e):
        return nn(hidden[index_of(level, e)], weight_of(level, e))

    def tok_part(level, d):
        weights = [w1[f, level] for f in range(4)]
        tiles = [tile_of(index1_rows[f : f + 1, level : level + 1], d) for f in range(4)]
        return nt(pre_grad[...], masked(weights, tiles))

    def out_box(slot, block):
        return out_in[slot, :, pl.ds(block * width, width)]

    def tok_box(slot, block):
        return tokens_in[slot, block]

    copies = []
    for side, inbox in enumerate((out_in, tokens_in)):
        copies.append([])
        for level, peer in enumerate((None, place.level(1), place.level(2), place.mp_peer(3), place.level(4))):
            if peer is None:
                copies[side].append(None)
                continue
            at = level - 1
            copies[side].append(
                [
                    remote(
                        sent.at[at, block],
                        inbox.at[at, block] if side else inbox.at[at, :, pl.ds(block * width, width)],
                        (x_send, x_recv),
                        (side, at, block),
                        peer,
                    )
                    for block in range(2)
                ]
            )

    parts = (out_part, tok_part)
    boxes = (out_box, tok_box)

    def send_parts(side):
        for level in (3, 4, 1):
            for block in range(2):
                if side:
                    copies[0][level][block].wait_send()
                sent[level - 1, block] = parts[side](level, block).astype(BF)
                copies[side][level][block].start()

    def send_joined(side):
        for block in range(2):
            copies[side][3][block].wait_recv()
            if side:
                copies[0][2][block].wait_send()
            joined = parts[side](2, block) + boxes[side](2, block).astype(F32)
            sent[1, block] = joined.astype(BF)
            copies[side][2][block].start()

    def join(side, rank_part, result):
        for block in range(2):
            total = parts[side](0, block) + rank_part(block)
            for level in (1, 4, 2):
                copies[side][level][block].wait_recv()
                total = total + boxes[side](level - 1, block).astype(F32)
            result[:, block * width : block * width + width] = total.astype(BF)

    send_parts(0)
    r_w1a.turn(0)
    sums_b.step_sum()
    send_joined(0)
    pl.semaphore_wait(inbox_free, 4)
    send_parts(1)
    r_sl.turn(2)
    r_w2.wait(2)
    eighth = r_w2.kept[2]
    swaps = [
        remote(
            g_w2.at[h, level, eighth[h], :],
            swap.at[h, level - 1],
            (swap_send, swap_recv),
            (h, level - 1),
            place.level(level),
        )
        for h in range(2)
        for level in range(1, 5)
    ]
    for copy in swaps:
        copy.start()
    r_w1b.turn(0)
    sums_b.step_back()
    r_w1a.turn(1)
    r_fr.turn(0)
    for copy in swaps:
        copy.wait()
    for h in range(2):
        for level in range(1, 5):
            g_w2[h, level, eighth[h], :] = swap[h, level - 1]
    r_w2.start(3)
    r_sl.turn(3)
    sums_b.finish()
    rank_second_t = ranks_b[0].T
    for h in range(2):
        g_sr[h, 0] = nn(rank_second_t[h * 256 : h * 256 + 256, :], out_grad[...]).astype(BF)
        g_fl[h, 0] = nn(tokens_t[0, h], ranks_b[1]).astype(BF)
    r_sr.start(0)
    r_fl.start(0)
    r_w1b.turn(1)
    send_joined(1)
    r_w2.turn(3)
    r_fr.turn(1)
    r_w1a.turn(2)
    r_sr.turn(0)
    r_fl.turn(0)
    join(0, lambda e: nn(ranks_b[0], second_right[:, e * width : e * width + width]), output)
    r_sl.turn(4)
    r_w2.turn(4)
    r_w1b.turn(2)
    r_w1a.turn(3)
    r_fr.turn(2)
    r_sr.turn(1)
    r_fl.turn(1)
    join(1, lambda d: nt(ranks_b[1], first_left[d * width : d * width + width, :]), tokens_grad)
    r_w1b.turn(3)
    r_w1a.turn(4)
    r_fr.turn(3)
    r_sr.turn(2)
    r_fl.turn(2)
    r_w1b.turn(4)
    r_fr.turn(4)
    r_sr.turn(3)
    r_fl.turn(3)
    r_sr.turn(4)
    r_fl.turn(4)
    for grad in (r_sl, r_w2, r_w1a, r_w1b, r_fr, r_sr, r_fl):
        grad.wait(5)
    for level in range(1, 5):
        for block in range(2):
            copies[1][level][block].wait_send()


def copy_kernel(*refs):
    count = (len(refs) - 1) // 2
    sems = refs[-1]
    copies = []
    for at in range(count):
        src, dst = refs[at], refs[count + at]
        step = src.shape[0] // 2
        for h in range(2):
            part = pl.ds(h * step, step)
            copies.append(
                pltpu.make_async_copy(src.at[part], dst.at[part], sems.at[len(copies)])
            )
    for copy in copies:
        copy.start()
    for copy in copies:
        copy.wait()


def body(
    tokens,
    out_grad,
    first_blocks,
    first_index,
    second_blocks,
    second_index,
    first_left,
    first_right,
    second_left,
    second_right,
):
    rows, features = tokens.shape
    rank = first_left.shape[1]
    units = first_right.shape[1]
    width = first_blocks.shape[2]
    vmem = pl.BlockSpec(memory_space=pltpu.VMEM)
    smem = pl.BlockSpec(memory_space=pltpu.SMEM)
    anywhere = pl.BlockSpec(memory_space=pl.ANY)
    dma = pltpu.SemaphoreType.DMA

    def shape(*extent):
        return jax.ShapeDtypeStruct(extent, BF)

    half = rank // 2
    index_sent = jnp.pad(second_index.T[:, None, :], ((0, 0), (0, 7), (0, 126)))
    grads = [
        (2, 5, width, width),
        (2, 1, units // 2, rank),
        (2, 10, width, width),
        (2, 1, rank // 2, units),
        (2, 1, rank // 2, features),
        (2, 1, features // 2, rank),
    ]
    pieces = grads[:2] + [(2, 5, width, width)] * 2 + grads[3:]
    inboxes = []
    for two, count, tall, wide in pieces:
        for step in (2, 4, 8):
            inboxes.append(pltpu.VMEM((two, count, tall // step, wide), BF))
    scratch = [
        pltpu.VMEM((features // width, rows, width), BF),
        pltpu.VMEM((4, features // width, rows, width), BF),
        pltpu.VMEM((4, rows, features), BF),
        pltpu.VMEM((4, 2, width, width), BF),
        pltpu.VMEM((4, 8, 128), jnp.int32),
        pltpu.SMEM((4, 8, 128), jnp.int32),
        pltpu.VMEM((units // width, rows, width), BF),
        pltpu.VMEM((units // width, width, rows), BF),
        pltpu.VMEM((rows, units), BF),
        pltpu.VMEM((5, features // width, width, rows), BF),
        pltpu.VMEM((rank, rows), BF),
        pltpu.VMEM((units // width, rows, width), F32),
        pltpu.VMEM((2, rows, half), F32),
        pltpu.VMEM((2, rows, half), BF),
        pltpu.VMEM((2, rows, half), BF),
    ]
    for _ in range(2):
        scratch += [
            pltpu.VMEM((2, rows, half), BF),
            pltpu.VMEM((7, 2, rows // 8, half), BF),
            pltpu.VMEM((2, rows, rank), BF),
        ]
    scratch += [
        pltpu.VMEM((2, 4, width // 8, width), BF),
        pltpu.VMEM((4, features // width, rows, width), BF),
        pltpu.VMEM((4, rows, features), BF),
    ]
    semaphores = [dma((2 + 2 * CHUNKS,))] * 4 + [dma((16,))] * 4 + [dma((4,))] * 4
    semaphores += [dma((7, 2, 6))] * 2 + [pltpu.SemaphoreType.REGULAR((7, 2))]
    semaphores += [dma((2, 4))] * 2 + [dma((2, 4, 2))] * 2
    semaphores += [pltpu.SemaphoreType.REGULAR, dma((2,))]
    results = pl.pallas_call(
        layer_kernel,
        out_shape=[shape(rows, features), shape(rows, features)]
        + [shape(*grads[at]) for at in (2, 5, 3, 0, 1, 4)],
        in_specs=[anywhere, vmem, vmem, smem, vmem, vmem, smem] + [vmem] * 5,
        out_specs=[vmem] * 8,
        scratch_shapes=scratch + inboxes + semaphores,
        compiler_params=pltpu.CompilerParams(
            collective_id=0, has_side_effects=True, vmem_limit_bytes=63 * 2**20
        ),
        name="layer_kernel",
    )(
        tokens,
        out_grad,
        first_blocks,
        first_index,
        first_index,
        second_blocks,
        second_index,
        index_sent,
        first_left,
        first_right,
        second_left,
        second_right,
    )
    output, tokens_grad, g_w1, g_fl, g_fr, g_w2, g_sl, g_sr = pl.pallas_call(
        copy_kernel,
        out_shape=[shape(*result.shape) for result in results],
        in_specs=[anywhere] * 8,
        out_specs=[anywhere] * 8,
        scratch_shapes=[dma((16,))],
        name="copy_kernel",
    )(*results)
    return (
        output,
        tokens_grad,
        g_w1.reshape(first_blocks.shape),
        g_fl.reshape(first_left.shape),
        g_fr.reshape(first_right.shape),
        g_w2.reshape(second_blocks.shape),
        g_sl.reshape(second_left.shape),
        g_sr.reshape(second_right.shape),
    )


def solution(mesh):
    placed = (
        P("dp", "mp"),
        P("dp", "mp"),
        P("mp", None, None, None),
        P("mp", None),
        P("mp", None, None, None),
        P("mp", None),
        P("mp", None),
        P(None, "mp"),
        P("mp", None),
        P(None, "mp"),
    )
    return jax.shard_map(
        body,
        mesh=mesh,
        in_specs=placed,
        out_specs=(
            P("dp", "mp"),
            P("dp", "mp"),
            P("mp", None, None, None),
            P("mp", None),
            P(None, "mp"),
            P("mp", None, None, None),
            P("mp", None),
            P(None, "mp"),
        ),
        check_vma=False,
    )
```

time: 728 us -> 512 us (0.70); the launches traced: 718 us -> 512 us
  Pallas kernels: 0 us -> 510 us
  blocking collectives: 444 us -> 0 us
  matrix products: 102 us -> 0 us
  waiting for transfers between devices: 75.4 us -> 0 us
  local copies, waits for them, and re-layouts: 73.5 us -> 1.38 us
  starting transfers between devices: 11.3 us -> 0 us
  other arithmetic: 9.83 us -> 0 us
    pallas_call x0 -> x2, Pallas kernels: none -> 510 us  [the longest x1 263 us: body(): pl.pallas_call(copy_kernel, out_shape=[shape(*result.shape) for result in...]
    psum x3 -> x0, blocking collectives: 444 us -> none  [the longest x1 286 us: body(): lax.psum((first_block_term, first_left_term, first_right_term), 'dp')]
    dot_general x38 -> x0, matrix products: 102 us -> none  [the longest x5 15.8 us: hidden_level(): return jnp.einsum('tej,ed->tdj', flow, hot)]
    ppermute x16 -> x0, waiting for transfers between devices: 75.4 us -> none  [partner(): return lax.ppermute(block, axis, route)]
    convert_element_type x2 -> x0, local copies, waits for them, and re-layouts: 23.8 us -> none  [the longest x1 13.1 us: body(): token_pick = jnp.einsum('tkdi,fkd->tfki', token_all, first_hot.astype(jnp...]
    unnamed x79 -> x0, local copies, waits for them, and re-layouts: 22.2 us -> none
    reshape x6 -> x0, local copies, waits for them, and re-layouts: 11.9 us -> none  [the longest x1 3.61 us: body(): block_first.reshape(tok_rows, -1)]
    ppermute x16 -> x0, starting transfers between devices: 11.3 us -> none  [partner(): return lax.ppermute(block, axis, route)]
  transfers between devices with their start and end apart: 16 -> 0, of which waited for: 3 -> 0; matrix products, arithmetic and copies ran while one was open for 17% -> 0% of each run, Pallas kernels for 0% -> 0%
where the time goes in v1:
time: 512 us
  Pallas kernels  510 us (100%)
    pallas_call x1, Pallas kernels, body(): pl.pallas_call(copy_kernel, out_shape=[shape(*result.shape) for result in...  263 us
    pallas_call x1, Pallas kernels, body(): pl.pallas_call(layer_kernel, out_shape=[shape(rows, features), shape(rows...  246 us

profile of v1, /device:TPU:0, one launch (start us, length us, event | category | flops | bytes accessed | tf_op | source)
XLA Modules:
  0.0 511.9 jit_solution(8405629210830017511)
XLA Ops:
  0.6 0.8 copy.18
  1.4 0.6 pad.4.index2_sent
  2.0 246.3 %layer_kernel.1 = (bf16[768,512]{1,0:T(8,128)(2,1)}, bf16[768,512]{1,0:T(8,128)(2,1)}, bf16[2,10,256,256]{3,2,1,0:T(8,128)(2,1)}, bf16[2,1,256,512]{3,2,1,0:T(8,...) custom-call(bf16[768,512]{1,0:T(8,128)(2,1)} %tokens.1, ...), custom_call_target="tpu_custom_call" | custom-call | tf_op jit(solution)/shard_map/layer_kernel/pallas_call | solution.py:757
  248.4 263.3 %copy_kernel.1 = (bf16[768,512]{1,0:T(8,128)(2,1)}, bf16[768,512]{1,0:T(8,128)(2,1)}, bf16[2,10,256,256]{3,2,1,0:T(8,128)(2,1)}, bf16[2,1,256,512]{3,2,1,0:T(8,1...) custom-call(bf16[768,512]{1,0:T(8,128)(2,1)} %get-tuple-element.24.r, ...), custom_call_target="tpu_custom_call" | custom-call | tf_op jit(solution)/shard_map/copy_kernel/pallas_call | solution.py:782

commit v2 on v1

v2 whole, which is shorter than its diff:
```python
import jax
import jax.numpy as jnp
from jax import lax
from jax.experimental import pallas as pl
from jax.experimental.pallas import tpu as pltpu
from jax.sharding import PartitionSpec as P

BF = jnp.bfloat16
F32 = jnp.float32
CHUNKS = 4


def nn(left, right):
    return jnp.dot(left, right, preferred_element_type=F32)


def nt(left, right):
    return lax.dot_general(left, right, (((1,), (1,)), ((), ())), preferred_element_type=F32)


def flip(bit, by):
    return 1 - bit if by else bit


def tile_of(index, at):
    hot = (index == at).astype(F32)
    return jnp.broadcast_to(hot, (16, 128)).astype(BF)


def masked(weights, tiles):
    parts = []
    for weight, tile in zip(weights, tiles):
        wide = jnp.concatenate([tile, tile], axis=1)
        tall = weight.reshape(weight.shape[0] // 16, 16, weight.shape[1])
        parts.append((tall * wide[None]).reshape(weight.shape))
    return jnp.concatenate(parts, axis=1)


class Place:
    def __init__(self):
        self.dp = lax.axis_index("dp")
        self.mp = lax.axis_index("mp")
        self.core = lax.rem(self.mp, 2)
        chip = lax.div(self.mp, 2)
        self.chip = chip
        self.y0 = lax.rem(chip, 2)
        self.y1 = lax.rem(lax.div(chip, 2), 2)
        self.z = lax.div(chip, 4)
        self.x0 = lax.rem(self.dp, 2)
        self.x1 = lax.rem(lax.div(self.dp, 2), 2)
        self.z_hi = lax.div(self.dp, 4)

    def mp_peer(self, chip_bits, core_bit=0):
        y0 = flip(self.y0, chip_bits & 1)
        y1 = flip(self.y1, chip_bits & 2)
        z = flip(self.z, chip_bits & 4)
        return (self.dp, ((z * 2 + y1) * 2 + y0) * 2 + flip(self.core, core_bit))

    def chip_peer(self, chip_bits):
        y0 = flip(self.y0, chip_bits & 1)
        y1 = flip(self.y1, chip_bits & 2)
        z = flip(self.z, chip_bits & 4)
        return (z * 2 + y1) * 2 + y0

    def dp_peer(self, bits):
        x0 = flip(self.x0, bits & 1)
        x1 = flip(self.x1, bits & 2)
        z = flip(self.z_hi, bits & 4)
        return ((z * 2 + x1) * 2 + x0, self.mp)

    def level(self, level):
        return [None, self.mp_peer(0, 1), self.mp_peer(1), self.mp_peer(2), self.mp_peer(4)][level]


def greet(peers):
    barrier = pltpu.get_barrier_semaphore()
    for peer in peers:
        pl.semaphore_signal(barrier, inc=1, device_id=peer, device_id_type=pl.DeviceIdType.MESH)
    pl.semaphore_wait(barrier, len(peers))


def remote(src, dst, sems, at, peer):
    send, recv = sems
    return pltpu.make_async_remote_copy(
        src_ref=src,
        dst_ref=dst,
        send_sem=send.at[at],
        recv_sem=recv.at[at],
        device_id=peer,
        device_id_type=pl.DeviceIdType.MESH,
    )


def at_ds(index, size):
    return pl.ds(pl.multiple_of(index * size, size), size)


def repeat(count, step):
    lax.fori_loop(0, count, lambda at, carry: (step(at), carry)[1], 0)


class RankSum:
    def __init__(self, place, rows, half, result, own, away, near, chip_sum, far, sems):
        self.place, self.result, self.sems = place, result, sems
        self.own, self.away, self.near, self.chip_sum, self.far = own, away, near, chip_sum, far
        self.part = rows // 8
        self.half = half
        self.columns = pl.ds(pl.multiple_of(place.core * half, half), half)
        self.rows = pl.ds(pl.multiple_of(place.chip * self.part, self.part), self.part)
        sibling = place.mp_peer(0, 1)
        self.cores = remote(away, near, sems, 0, sibling)
        self.scatter = []
        self.gather = []
        for bits in range(1, 8):
            other = pl.ds(pl.multiple_of(place.chip_peer(bits) * self.part, self.part), self.part)
            peer = place.mp_peer(bits)
            self.scatter.append(
                remote(chip_sum.at[:, other, :], far.at[bits - 1], sems, bits, peer)
            )
            mine = result.at[:, self.rows, self.columns]
            self.gather.append(remote(mine, mine, sems, 7 + bits, peer))
        whole = result.at[:, :, self.columns]
        self.back = remote(whole, whole, sems, 15, sibling)

    def set(self, which, own, away):
        self.own[which] = own
        self.away[which] = away.astype(BF)

    def start(self):
        self.cores.start()

    def step_chip(self):
        self.cores.wait()
        for which in range(2):
            self.chip_sum[which] = (self.own[which] + self.near[which].astype(F32)).astype(BF)
        for copy in self.scatter:
            copy.start()

    def step_sum(self):
        total = self.chip_sum[:, self.rows, :].astype(F32)
        for copy in self.scatter:
            copy.wait()
        for bits in range(7):
            total = total + self.far[bits].astype(F32)
        self.result[:, self.rows, self.columns] = total.astype(BF)
        for copy in self.gather:
            copy.start()

    def step_back(self):
        for copy in self.gather:
            copy.wait()
        self.back.start()

    def finish(self):
        self.back.wait()


class Spread:
    def __init__(self, place, held, sems):
        self.held, self.sems = held, sems
        self.blocked = len(held.shape) == 4
        self.rows = held.shape[-2] * (2 if self.blocked else 1) // CHUNKS
        self.one, self.two, self.three = place.level(1), place.level(2), place.mp_peer(3)
        self.four = place.level(4)
        self.direct = [
            remote(held.at[0], held.at[level], sems, at, peer)
            for at, (level, peer) in enumerate(((4, self.four), (1, self.one)))
        ]

    def piece(self, slot, chunk):
        if self.blocked:
            return self.held.at[slot, lax.div(chunk, 2), at_ds(lax.rem(chunk, 2), self.rows), :]
        return self.held.at[slot, at_ds(chunk, self.rows), :]

    def near(self, chunk):
        return remote(
            self.piece(0, chunk), self.piece(2, chunk), self.sems, 2 + chunk, self.two
        )

    def onward(self, chunk):
        return remote(
            self.piece(2, chunk), self.piece(3, chunk), self.sems, 2 + CHUNKS + chunk, self.three
        )

    def start_direct(self):
        for copy in self.direct:
            copy.start()

    def start_near(self, first, count):
        repeat(count, lambda at: self.near(first + at).start())

    def pass_on(self, chunk):
        chunk = jnp.int32(chunk)
        self.near(chunk).wait_recv()
        self.onward(chunk).start()

    def wait_direct(self):
        for copy in self.direct:
            copy.wait_recv()

    def wait_onward(self):
        repeat(CHUNKS, lambda chunk: self.onward(chunk).wait_recv())

    def close(self):
        for copy in self.direct:
            copy.wait_send()

        def finish(chunk):
            self.near(chunk).wait_send()
            self.onward(chunk).wait_send()

        repeat(CHUNKS, finish)


class Reduced:
    def __init__(self, place, grad, lead, first, second, third, sems, credit, at):
        self.credit, self.at, self.lead = credit, at, lead
        blocks = pl.ds(lead, first.shape[1])
        self.grad, self.bufs = grad, (first, second, third)
        rows = grad.shape[2]
        x0, x1 = place.x0, place.x1
        cross = x0 + x1 - 2 * x0 * x1
        near, back, far = place.dp_peer(1), place.dp_peer(3), place.dp_peer(4)
        self.greeted = (near, back)
        self.steps = [[] for _ in range(5)]
        self.kept = [[] for _ in range(3)]
        for h in range(2):
            keys = (cross, x1) if h == 0 else (x1, x0)
            peers = (near, back) if h == 0 else (back, near)
            offset, size = 0, rows
            for step in range(2):
                size = size // 2
                keep = pl.ds(pl.multiple_of(offset + keys[step] * size, size), size)
                send = pl.ds(pl.multiple_of(offset + (1 - keys[step]) * size, size), size)
                self.kept[step].append(keep)
                self.steps[step].append(
                    remote(
                        grad.at[h, blocks, send, :],
                        self.bufs[step].at[h],
                        sems,
                        (at, h, step),
                        peers[step],
                    )
                )
                own = grad.at[h, blocks, keep, :]
                self.steps[4 - step].append(
                    remote(own, own, sems, (at, h, 4 - step), peers[step])
                )
                offset = offset + keys[step] * size
            self.kept[2].append(self.kept[1][h])
            self.steps[2].append(
                remote(
                    grad.at[h, blocks, self.kept[1][h], :],
                    self.bufs[2].at[h],
                    sems,
                    (at, h, 2),
                    far,
                )
            )

    def start(self, step):
        if step == 3:
            pl.semaphore_wait(self.credit.at[self.at], 2)
        for copy in self.steps[step]:
            copy.start()

    def turn(self, step):
        self.wait(step)
        self.start(step + 1)

    def wait(self, step):
        for h, copy in enumerate(self.steps[step]):
            copy.wait()
            if step < 3:
                keep, buf = self.kept[step][h], self.bufs[step]

                def add(n):
                    self.grad[h, self.lead + n, keep, :] = (
                        self.grad[h, self.lead + n, keep, :].astype(F32) + buf[h, n].astype(F32)
                    ).astype(BF)

                repeat(buf.shape[1], add)
        if step == 1:
            for peer in self.greeted:
                pl.semaphore_signal(
                    self.credit.at[self.at],
                    inc=1,
                    device_id=peer,
                    device_id_type=pl.DeviceIdType.MESH,
                )


def layer_kernel(
    tokens,
    out_grad,
    w1,
    index1,
    index1_rows,
    w2,
    index2_sent,
    first_left,
    first_right,
    second_left,
    second_right,
    output,
    tokens_grad,
    g_w1,
    g_fl,
    g_fr,
    g_w2,
    g_sl,
    g_sr,
    tokens_all,
    grads_all,
    w2_all,
    index_all,
    index_smem,
    hidden,
    hidden_t,
    pre_grad,
    tokens_t,
    rank_first_t,
    slope,
    own,
    away,
    chip_sum,
    near_a,
    far_a,
    ranks_a,
    near_b,
    far_b,
    ranks_b,
    swap,
    sent,
    out_in,
    *rest,
):
    bufs, rest = rest[:21], rest[21:]
    (
        tok_send,
        tok_recv,
        grad_send,
        grad_recv,
        rank_send_a,
        rank_recv_a,
        rank_send_b,
        rank_recv_b,
        w_send,
        w_recv,
        i_send,
        i_recv,
        dp_send,
        dp_recv,
        credit,
        swap_send,
        swap_recv,
        x_send,
        x_recv,
        inbox_free,
        local,
    ) = rest
    place = Place()
    rows = pre_grad.shape[0]
    half = first_left.shape[1] // 2
    width = w1.shape[2]
    mine = pl.ds(pl.multiple_of(place.core * half, half), half)
    other = pl.ds(pl.multiple_of((1 - place.core) * half, half), half)

    loads = [
        pltpu.make_async_copy(
            tokens.at[:, pl.ds(d * width, width)], tokens_all.at[0, d], local.at[d]
        )
        for d in range(2)
    ]
    loads.append(pltpu.make_async_copy(out_grad, grads_all.at[0], local.at[2]))
    loads.append(pltpu.make_async_copy(w2.at[:, 0], w2_all.at[0], local.at[3]))
    loads.append(pltpu.make_async_copy(index2_sent.at[0], index_all.at[0], local.at[4]))
    for load in loads:
        load.start()
    greet(
        [place.mp_peer(bits) for bits in range(1, 8)]
        + [place.mp_peer(0, 1)]
        + [place.dp_peer(bits) for bits in (1, 3, 4)]
    )
    spread_tok = Spread(place, tokens_all, (tok_send, tok_recv))
    spread_grad = Spread(place, grads_all, (grad_send, grad_recv))
    sums_a = RankSum(
        place, rows, half, ranks_a, own, away, near_a, chip_sum, far_a, (rank_send_a, rank_recv_a)
    )
    sums_b = RankSum(
        place, rows, half, ranks_b, own, away, near_b, chip_sum, far_b, (rank_send_b, rank_recv_b)
    )
    w_copies = [
        remote(w2.at[:, level], w2_all.at[level], (w_send, w_recv), level - 1, place.level(level))
        for level in (4, 2, 3, 1)
    ]
    i_copies = [
        remote(
            index2_sent.at[level],
            index_all.at[level],
            (i_send, i_recv),
            level - 1,
            place.level(level),
        )
        for level in range(1, 5)
    ]
    dp_sems = (dp_send, dp_recv)
    grads = ((g_w2, 0), (g_sl, 0), (g_w1, 0), (g_w1, 5), (g_fr, 0), (g_sr, 0), (g_fl, 0))
    r_w2, r_sl, r_w1a, r_w1b, r_fr, r_sr, r_fl = [
        Reduced(place, grad, lead, *bufs[3 * at : 3 * at + 3], dp_sems, credit, at)
        for at, (grad, lead) in enumerate(grads)
    ]

    def turn_tokens(level):
        def step(d):
            tokens_t[level, d] = tokens_all[level, d].T

        repeat(2, step)

    for load in loads:
        load.wait()
    spread_tok.start_near(0, CHUNKS)
    spread_tok.start_direct()
    for copy in i_copies:
        copy.start()
    both = jnp.concatenate([tokens_all[0, 0], tokens_all[0, 1]], axis=1)
    sums_a.set(0, nn(both, first_left[:, mine]), nn(both, first_left[:, other]))
    flow = grads_all[0]
    sums_a.set(1, nt(flow, second_right[mine, :]), nt(flow, second_right[other, :]))
    sums_a.start()
    turn_tokens(0)
    spread_tok.pass_on(0)
    sums_a.step_chip()
    spread_tok.pass_on(1)
    spread_tok.pass_on(2)
    spread_grad.start_near(0, 2)
    spread_grad.start_direct()
    spread_tok.pass_on(3)
    spread_grad.start_near(2, 2)
    for copy in w_copies:
        copy.start()
    sums_a.step_sum()
    spread_tok.wait_direct()
    turn_tokens(1)
    turn_tokens(4)
    sums_a.step_back()
    turn_tokens(2)
    spread_grad.pass_on(0)
    spread_tok.wait_onward()
    turn_tokens(3)
    sums_a.finish()
    rank_first_t[...] = ranks_a[0].T

    def forward(f):
        columns = at_ds(f, width)
        picks = [tokens_all[level, index1[f, level]] for level in range(5)]
        pre = nn(jnp.concatenate(picks, axis=1), w1[f].reshape(5 * width, width))
        pre = pre + nn(ranks_a[0], first_right[:, columns])
        sigma = 1.0 / (1.0 + jnp.exp(-pre))
        active = (pre * sigma).astype(BF)
        hidden[f] = active
        hidden_t[f] = active.T
        slope[f] = sigma * (1.0 + pre * (1.0 - sigma))

    def forward_and_pass(f):
        forward(f)
        spread_grad.pass_on(f + 1)

    repeat(3, forward_and_pass)
    forward(jnp.int32(3))
    spread_tok.close()
    for peer in (place.level(1), place.level(2), place.mp_peer(3), place.level(4)):
        pl.semaphore_signal(inbox_free, inc=1, device_id=peer, device_id_type=pl.DeviceIdType.MESH)

    for copy in i_copies + w_copies:
        copy.wait()
    fetch = pltpu.make_async_copy(index_all, index_smem, local.at[0])
    fetch.start()
    fetch.wait()
    spread_grad.wait_direct()

    def second_left_part(d):
        g_sl[lax.div(d, 2), 0, at_ds(lax.rem(d, 2), width), :] = nn(hidden_t[d], ranks_a[1]).astype(BF)

    repeat(4, second_left_part)
    r_sl.start(0)

    def second_grads(at):
        level = at + lax.div(at, 3)
        for e in range(2):
            flow = grads_all[level, :, e * width : e * width + width]
            g_w2[e, level] = nn(hidden_t[index_smem[level, 0, e]], flow).astype(BF)

    repeat(4, second_grads)
    spread_grad.wait_onward()
    for e in range(2):
        flow = grads_all[3, :, e * width : e * width + width]
        g_w2[e, 3] = nn(hidden_t[index_smem[3, 0, e]], flow).astype(BF)
    r_w2.start(0)

    def hidden_back(d):
        total = nt(ranks_a[1], second_left[at_ds(d, width), :])
        for level in range(5):
            weights = [w2_all[level, e] for e in range(2)]
            tiles = [tile_of(index_all[level, 0:1, e : e + 1], d) for e in range(2)]
            total = total + nt(grads_all[level], masked(weights, tiles))
        pre_grad[:, at_ds(d, width)] = (total * slope[d]).astype(BF)

    repeat(4, hidden_back)
    spread_grad.close()
    r_sl.turn(0)
    r_w2.turn(0)

    units = jnp.concatenate([hidden[d] for d in range(4)], axis=1)
    sums_b.set(0, nn(units, second_left[:, mine]), nn(units, second_left[:, other]))
    sums_b.set(1, nt(pre_grad[...], first_right[mine, :]), nt(pre_grad[...], first_right[other, :]))
    sums_b.start()

    def first_grads(part):
        def step(h):
            f = 2 * h + part
            picks = [tokens_t[level, index1[f, level]] for level in range(5)]
            product = nn(
                jnp.concatenate(picks + [rank_first_t[...]], axis=0),
                pre_grad[:, at_ds(f, width)],
            ).astype(BF)
            for level in range(5):
                g_w1[h, part * 5 + level] = product[level * width : level * width + width]
            for r in range(2):
                low = (5 + r) * width
                g_fr[r, 0, :, at_ds(f, width)] = product[low : low + width]

        repeat(2, step)

    first_grads(0)
    r_w1a.start(0)
    sums_b.step_chip()
    first_grads(1)
    r_w1b.start(0)
    r_fr.start(0)
    r_sl.turn(1)
    r_w2.turn(1)

    def out_part(level, e):
        return nn(hidden[index_smem[level, 0, e]], w2_all[level, e])

    def tok_part(level, d):
        weights = [w1[f, level] for f in range(4)]
        tiles = [tile_of(index1_rows[level, 0:1, pl.ds(f, 1)], d) for f in range(4)]
        return nt(pre_grad[...], masked(weights, tiles))

    parts = (out_part, tok_part)

    def box(side, slot, block):
        return tokens_all.at[slot, block] if side else out_in.at[slot, block]

    def remote_part(side, level, peer):
        return remote(
            sent.at[level],
            tokens_all.at[level] if side else out_in.at[level],
            (x_send, x_recv),
            (side, level),
            peer,
        )

    peers = {1: place.level(1), 2: place.level(2), 3: place.mp_peer(3), 4: place.level(4)}
    copies = [
        {level: remote_part(side, level, peer) for level, peer in peers.items()}
        for side in range(2)
    ]

    def send_parts(side):
        for level in (3, 4, 1):
            if side:
                copies[0][level].wait_send()

            def step(block, level=level):
                sent[level, block] = parts[side](level, block).astype(BF)

            repeat(2, step)
            copies[side][level].start()

    def send_joined(side):
        copies[side][3].wait_recv()
        if side:
            copies[0][2].wait_send()

        def step(block):
            joined = parts[side](2, block) + box(side, 3, block)[...].astype(F32)
            sent[2, block] = joined.astype(BF)

        repeat(2, step)
        copies[side][2].start()

    def join(side, rank_part, result):
        for level in (1, 4, 2):
            copies[side][level].wait_recv()

        def step(block):
            total = parts[side](0, block) + rank_part(block)
            for level in (1, 4, 2):
                total = total + box(side, level, block)[...].astype(F32)
            result[:, at_ds(block, width)] = total.astype(BF)

        repeat(2, step)

    send_parts(0)
    r_w1a.turn(0)
    sums_b.step_sum()
    send_joined(0)
    pl.semaphore_wait(inbox_free, 4)
    r_sl.turn(2)
    r_w2.wait(2)
    quarter = r_w2.kept[2]
    swaps = [
        remote(
            g_w2.at[h, level, quarter[h], :],
            swap.at[h, level - 1],
            (swap_send, swap_recv),
            (h, level - 1),
            place.level(level),
        )
        for h in range(2)
        for level in range(1, 5)
    ]
    for copy in swaps:
        copy.start()
    send_parts(1)
    r_w1b.turn(0)
    sums_b.step_back()
    r_w1a.turn(1)
    r_fr.turn(0)
    for copy in swaps:
        copy.wait()
    for h in range(2):
        for level in range(1, 5):
            g_w2[h, level, quarter[h], :] = swap[h, level - 1]
    r_w2.start(3)
    sums_b.finish()
    rank_second_t = ranks_b[0].T
    for h in range(2):
        g_sr[h, 0] = nn(rank_second_t[h * 256 : h * 256 + 256, :], grads_all[0]).astype(BF)
        g_fl[h, 0] = nn(tokens_t[0, h], ranks_b[1]).astype(BF)
    r_sr.start(0)
    r_fl.start(0)
    r_w1b.turn(1)
    r_sl.turn(3)
    send_joined(1)
    r_fr.turn(1)
    r_w1a.turn(2)
    r_w2.turn(3)
    r_sr.turn(0)
    r_fl.turn(0)
    join(0, lambda e: nn(ranks_b[0], second_right[:, at_ds(e, width)]), output)
    r_w1b.turn(2)
    r_sr.turn(1)
    r_fl.turn(1)
    r_fr.turn(2)
    r_w1a.turn(3)
    join(1, lambda d: nt(ranks_b[1], first_left[at_ds(d, width), :]), tokens_grad)
    r_sr.turn(2)
    r_fl.turn(2)
    r_w1b.turn(3)
    r_fr.turn(3)
    r_sr.turn(3)
    r_fl.turn(3)
    for grad in (r_sl, r_w2, r_w1a, r_w1b, r_fr, r_sr, r_fl):
        grad.wait(4)
    for level in range(1, 5):
        copies[1][level].wait_send()


def copy_kernel(*refs):
    count = len(refs) // 2
    for at in range(count):
        refs[count + at][...] = refs[at][...]


def body(
    tokens,
    out_grad,
    first_blocks,
    first_index,
    second_blocks,
    second_index,
    first_left,
    first_right,
    second_left,
    second_right,
):
    rows, features = tokens.shape
    rank = first_left.shape[1]
    units = first_right.shape[1]
    width = first_blocks.shape[2]
    vmem = pl.BlockSpec(memory_space=pltpu.VMEM)
    smem = pl.BlockSpec(memory_space=pltpu.SMEM)
    anywhere = pl.BlockSpec(memory_space=pl.ANY)
    dma = pltpu.SemaphoreType.DMA

    def shape(*extent):
        return jax.ShapeDtypeStruct(extent, BF)

    half = rank // 2

    def rows_of(index):
        wide = 128 - index.shape[0]
        return jnp.pad(index.T[:, None, :], ((0, 0), (0, 7), (0, wide)))

    grads = [
        (2, 5, width, width),
        (2, 1, units // 2, rank),
        (2, 10, width, width),
        (2, 1, rank // 2, units),
        (2, 1, rank // 2, features),
        (2, 1, features // 2, rank),
    ]
    pieces = grads[:2] + [(2, 5, width, width)] * 2 + grads[3:]
    inboxes = []
    for two, count, tall, wide in pieces:
        for step in (2, 4, 4):
            inboxes.append(pltpu.VMEM((two, count, tall // step, wide), BF))
    scratch = [
        pltpu.VMEM((5, features // width, rows, width), BF),
        pltpu.VMEM((5, rows, features), BF),
        pltpu.VMEM((5, 2, width, width), BF),
        pltpu.VMEM((5, 8, 128), jnp.int32),
        pltpu.SMEM((5, 8, 128), jnp.int32),
        pltpu.VMEM((units // width, rows, width), BF),
        pltpu.VMEM((units // width, width, rows), BF),
        pltpu.VMEM((rows, units), BF),
        pltpu.VMEM((5, features // width, width, rows), BF),
        pltpu.VMEM((rank, rows), BF),
        pltpu.VMEM((units // width, rows, width), F32),
        pltpu.VMEM((2, rows, half), F32),
        pltpu.VMEM((2, rows, half), BF),
        pltpu.VMEM((2, rows, half), BF),
    ]
    for _ in range(2):
        scratch += [
            pltpu.VMEM((2, rows, half), BF),
            pltpu.VMEM((7, 2, rows // 8, half), BF),
            pltpu.VMEM((2, rows, rank), BF),
        ]
    scratch += [
        pltpu.VMEM((2, 4, width // 4, width), BF),
        pltpu.VMEM((5, features // width, rows, width), BF),
        pltpu.VMEM((5, features // width, rows, width), BF),
    ]
    semaphores = [dma((2 + 2 * CHUNKS,))] * 4 + [dma((16,))] * 4 + [dma((4,))] * 4
    semaphores += [dma((7, 2, 5))] * 2 + [pltpu.SemaphoreType.REGULAR((7,))]
    semaphores += [dma((2, 4))] * 2 + [dma((2, 5))] * 2
    semaphores += [pltpu.SemaphoreType.REGULAR, dma((5,))]
    order = (2, 5, 3, 0, 1, 4)
    results = pl.pallas_call(
        layer_kernel,
        out_shape=[shape(rows, features), shape(rows, features)]
        + [shape(*grads[at]) for at in order],
        in_specs=[anywhere, anywhere, vmem, smem, vmem, anywhere, anywhere] + [vmem] * 4,
        out_specs=[vmem] * 8,
        scratch_shapes=scratch + inboxes + semaphores,
        compiler_params=pltpu.CompilerParams(
            collective_id=0, has_side_effects=True, vmem_limit_bytes=63 * 2**20
        ),
        name="layer_kernel",
    )(
        tokens,
        out_grad,
        first_blocks,
        first_index,
        rows_of(first_index),
        second_blocks,
        rows_of(second_index),
        first_left,
        first_right,
        second_left,
        second_right,
    )
    flat = [result.reshape(-1, result.shape[-1]) for result in results]
    steps = 4
    specs = [
        pl.BlockSpec((result.shape[0] // steps, result.shape[1]), lambda at: (at, 0))
        for result in flat
    ]
    output, tokens_grad, g_w1, g_fl, g_fr, g_w2, g_sl, g_sr = pl.pallas_call(
        copy_kernel,
        out_shape=[shape(*result.shape) for result in flat],
        grid=(steps,),
        in_specs=specs,
        out_specs=specs,
        compiler_params=pltpu.CompilerParams(vmem_limit_bytes=32 * 2**20),
        name="copy_kernel",
    )(*flat)
    return (
        output,
        tokens_grad,
        g_w1.reshape(first_blocks.shape),
        g_fl.reshape(first_left.shape),
        g_fr.reshape(first_right.shape),
        g_w2.reshape(second_blocks.shape),
        g_sl.reshape(second_left.shape),
        g_sr.reshape(second_right.shape),
    )


def solution(mesh):
    placed = (
        P("dp", "mp"),
        P("dp", "mp"),
        P("mp", None, None, None),
        P("mp", None),
        P("mp", None, None, None),
        P("mp", None),
        P("mp", None),
        P(None, "mp"),
        P("mp", None),
        P(None, "mp"),
    )
    return jax.shard_map(
        body,
        mesh=mesh,
        in_specs=placed,
        out_specs=(
            P("dp", "mp"),
            P("dp", "mp"),
            P("mp", None, None, None),
            P("mp", None),
            P(None, "mp"),
            P("mp", None, None, None),
            P("mp", None),
            P(None, "mp"),
        ),
        check_vma=False,
    )
```

time: 512 us -> 255 us (0.50)
  Pallas kernels: 510 us -> 241 us
  local copies, waits for them, and re-layouts: 1.38 us -> 12.6 us
    pallas_call x1, Pallas kernels: 263 us -> 3.58 us  [body(): pl.pallas_call(copy_kernel, out_shape=[shape(*result.shape) for result in...]
    unnamed x0 -> x16, local copies, waits for them, and re-layouts: none -> 9.84 us
    pallas_call x1, Pallas kernels: 246 us -> 238 us  [body(): pl.pallas_call(layer_kernel, out_shape=[shape(rows, features), shape(rows...]
where the time goes in v2:
time: 255 us
  Pallas kernels  241 us (95%)
  local copies, waits for them, and re-layouts  12.6 us (5%)
    pallas_call x1, Pallas kernels, body(): pl.pallas_call(layer_kernel, out_shape=[shape(rows, features), shape(rows...  238 us
    unnamed x16, local copies, waits for them, and re-layouts  9.84 us

profile of v2, /device:TPU:0, one launch (start us, length us, event | category | flops | bytes accessed | tf_op | source)
XLA Modules:
  0.0 254.6 jit_solution(16640167578236880512)
XLA Ops:
  0.6 0.8 copy.19
  1.4 0.8 copy.18
  2.2 0.6 pad.8.index1_rows
  2.8 0.6 pad.9.index2_sent
  3.4 237.7 %layer_kernel.1 = (bf16[768,512]{1,0:T(8,128)(2,1)}, bf16[768,512]{1,0:T(8,128)(2,1)}, bf16[2,10,256,256]{3,2,1,0:T(8,128)(2,1)}, bf16[2,1,256,512]{3,2,1,0:T(8,...) custom-call(bf16[768,512]{1,0:T(8,128)(2,1)} %tokens.1, ...), custom_call_target="tpu_custom_call" | custom-call | tf_op jit(solution)/shard_map/layer_kernel/pallas_call | solution.py:754
  241.1 0.0 copy-start
  241.1 1.7 copy-done
  242.8 0.0 copy-start.1
  242.8 1.3 copy-done.1
  244.1 0.0 copy-start.2
  244.1 1.2 copy-done.2
  245.4 0.0 copy-start.3
  245.4 1.2 copy-done.3
  246.6 0.0 copy-start.4
  246.6 1.1 copy-done.4
  247.7 0.0 copy-start.5
  247.7 1.1 copy-done.5
  248.9 0.0 copy-start.6
  248.9 1.0 copy-done.6
  249.9 0.0 copy-start.7
  249.9 1.0 copy-done.7
  250.9 3.6 %copy_kernel.1 = (bf16[768,512]{1,0:T(8,128)(2,1)}, bf16[768,512]{1,0:T(8,128)(2,1)}, bf16[5120,256]{1,0:T(8,128)(2,1)}, bf16[512,512]{1,0:T(8,128)(2,1)}, bf16[...) custom-call(bf16[768,512]{1,0:T(8,128)(2,1)S(1)} %copy-done.4, ...), custom_call_target="tpu_custom_call" | custom-call | tf_op jit(solution)/shard_map/copy_kernel/pallas_call | solution.py:784
Async XLA Ops:
  241.1 1.7 copy-start
  242.8 1.3 copy-start.1
  244.1 1.2 copy-start.2
  245.4 1.2 copy-start.3
  246.6 1.1 copy-start.4
  247.7 1.1 copy-start.5
  248.9 1.0 copy-start.6
  249.9 1.0 copy-start.7

commit v3 on v2

--- a/solution.py
+++ b/solution.py
@@ -68,6 +68,9 @@
         z = flip(self.z_hi, bits & 4)
         return ((z * 2 + x1) * 2 + x0, self.mp)
 
+    def far_z(self):
+        return (self.dp_peer(4)[0], self.mp_peer(4)[1])
+
     def level(self, level):
         return [None, self.mp_peer(0, 1), self.mp_peer(1), self.mp_peer(2), self.mp_peer(4)][level]
 
@@ -100,27 +103,29 @@
 
 
 class RankSum:
-    def __init__(self, place, rows, half, result, own, away, near, chip_sum, far, sems):
-        self.place, self.result, self.sems = place, result, sems
+    def __init__(self, place, result, own, away, near, chip_sum, far, part, z_part, sems):
+        self.result = result
         self.own, self.away, self.near, self.chip_sum, self.far = own, away, near, chip_sum, far
-        self.part = rows // 8
-        self.half = half
-        self.columns = pl.ds(pl.multiple_of(place.core * half, half), half)
-        self.rows = pl.ds(pl.multiple_of(place.chip * self.part, self.part), self.part)
+        self.part, self.z_part = part, z_part
+        rows, half = near.shape[1], near.shape[2]
+        step = rows // 4
+        self.columns = at_ds(place.core, half)
+        self.rows = at_ds(place.y1 * 2 + place.y0, step)
         sibling = place.mp_peer(0, 1)
         self.cores = remote(away, near, sems, 0, sibling)
         self.scatter = []
         self.gather = []
-        for bits in range(1, 8):
-            other = pl.ds(pl.multiple_of(place.chip_peer(bits) * self.part, self.part), self.part)
+        mine = result.at[:, self.rows, self.columns]
+        for bits in range(1, 4):
+            other = at_ds(flip(place.y1, bits & 2) * 2 + flip(place.y0, bits & 1), step)
             peer = place.mp_peer(bits)
             self.scatter.append(
                 remote(chip_sum.at[:, other, :], far.at[bits - 1], sems, bits, peer)
             )
-            mine = result.at[:, self.rows, self.columns]
-            self.gather.append(remote(mine, mine, sems, 7 + bits, peer))
+            self.gather.append(remote(mine, mine, sems, 3 + bits, peer))
+        self.across = remote(part, z_part, sems, 7, place.level(4))
         whole = result.at[:, :, self.columns]
-        self.back = remote(whole, whole, sems, 15, sibling)
+        self.back = remote(whole, whole, sems, 8, sibling)
 
     def set(self, which, own, away):
         self.own[which] = own
@@ -131,17 +136,26 @@
 
     def step_chip(self):
         self.cores.wait()
-        for which in range(2):
+
+        def add(which):
             self.chip_sum[which] = (self.own[which] + self.near[which].astype(F32)).astype(BF)
+
+        repeat(2, add)
         for copy in self.scatter:
             copy.start()
 
-    def step_sum(self):
+    def step_across(self):
         total = self.chip_sum[:, self.rows, :].astype(F32)
         for copy in self.scatter:
             copy.wait()
-        for bits in range(7):
-            total = total + self.far[bits].astype(F32)
+        for at in range(3):
+            total = total + self.far[at].astype(F32)
+        self.part[...] = total.astype(BF)
+        self.across.start()
+
+    def step_sum(self):
+        self.across.wait()
+        total = self.part[...].astype(F32) + self.z_part[...].astype(F32)
         self.result[:, self.rows, self.columns] = total.astype(BF)
         for copy in self.gather:
             copy.start()
@@ -213,14 +227,16 @@
 
 
 class Reduced:
-    def __init__(self, place, grad, lead, first, second, third, sems, credit, at):
+    def __init__(self, place, grad, lead, first, second, third, relay, sems, credit, at):
         self.credit, self.at, self.lead = credit, at, lead
         blocks = pl.ds(lead, first.shape[1])
         self.grad, self.bufs = grad, (first, second, third)
         rows = grad.shape[2]
         x0, x1 = place.x0, place.x1
         cross = x0 + x1 - 2 * x0 * x1
-        near, back, far = place.dp_peer(1), place.dp_peer(3), place.dp_peer(4)
+        near, back = place.dp_peer(1), place.dp_peer(3)
+        by_z = (place.level(4), place.far_z())
+        self.passed = []
         self.greeted = (near, back)
         self.steps = [[] for _ in range(5)]
         self.kept = [[] for _ in range(3)]
@@ -250,12 +266,11 @@
             self.kept[2].append(self.kept[1][h])
             self.steps[2].append(
                 remote(
-                    grad.at[h, blocks, self.kept[1][h], :],
-                    self.bufs[2].at[h],
-                    sems,
-                    (at, h, 2),
-                    far,
+                    grad.at[h, blocks, self.kept[1][h], :], relay.at[h], sems, (at, h, 2), by_z[h]
                 )
+            )
+            self.passed.append(
+                remote(relay.at[h], self.bufs[2].at[h], sems, (at, h, 5), by_z[1 - h])
             )
 
     def start(self, step):
@@ -268,9 +283,18 @@
         self.wait(step)
         self.start(step + 1)
 
+    def relay(self):
+        for copy, onward in zip(self.steps[2], self.passed):
+            copy.wait_recv()
+            onward.start()
+
     def wait(self, step):
         for h, copy in enumerate(self.steps[step]):
-            copy.wait()
+            if step == 2:
+                copy.wait_send()
+                self.passed[h].wait()
+            else:
+                copy.wait()
             if step < 3:
                 keep, buf = self.kept[step][h], self.bufs[step]
 
@@ -295,9 +319,8 @@
     out_grad,
     w1,
     index1,
-    index1_rows,
     w2,
-    index2_sent,
+    table,
     first_left,
     first_right,
     second_left,
@@ -324,18 +347,21 @@
     own,
     away,
     chip_sum,
+    part,
     near_a,
     far_a,
+    z_a,
     ranks_a,
     near_b,
     far_b,
+    z_b,
     ranks_b,
     swap,
     sent,
     out_in,
     *rest,
 ):
-    bufs, rest = rest[:21], rest[21:]
+    bufs, rest = rest[:28], rest[28:]
     (
         tok_send,
         tok_recv,
@@ -374,21 +400,21 @@
     ]
     loads.append(pltpu.make_async_copy(out_grad, grads_all.at[0], local.at[2]))
     loads.append(pltpu.make_async_copy(w2.at[:, 0], w2_all.at[0], local.at[3]))
-    loads.append(pltpu.make_async_copy(index2_sent.at[0], index_all.at[0], local.at[4]))
+    loads.append(pltpu.make_async_copy(table, index_all.at[0], local.at[4]))
     for load in loads:
         load.start()
     greet(
         [place.mp_peer(bits) for bits in range(1, 8)]
         + [place.mp_peer(0, 1)]
-        + [place.dp_peer(bits) for bits in (1, 3, 4)]
+        + [place.dp_peer(1), place.dp_peer(3), place.far_z()]
     )
     spread_tok = Spread(place, tokens_all, (tok_send, tok_recv))
     spread_grad = Spread(place, grads_all, (grad_send, grad_recv))
     sums_a = RankSum(
-        place, rows, half, ranks_a, own, away, near_a, chip_sum, far_a, (rank_send_a, rank_recv_a)
+        place, ranks_a, own, away, near_a, chip_sum, far_a, part, z_a, (rank_send_a, rank_recv_a)
     )
     sums_b = RankSum(
-        place, rows, half, ranks_b, own, away, near_b, chip_sum, far_b, (rank_send_b, rank_recv_b)
+        place, ranks_b, own, away, near_b, chip_sum, far_b, part, z_b, (rank_send_b, rank_recv_b)
     )
     w_copies = [
         remote(w2.at[:, level], w2_all.at[level], (w_send, w_recv), level - 1, place.level(level))
@@ -396,7 +422,7 @@
     ]
     i_copies = [
         remote(
-            index2_sent.at[level],
+            table,
             index_all.at[level],
             (i_send, i_recv),
             level - 1,
@@ -407,7 +433,7 @@
     dp_sems = (dp_send, dp_recv)
     grads = ((g_w2, 0), (g_sl, 0), (g_w1, 0), (g_w1, 5), (g_fr, 0), (g_sr, 0), (g_fl, 0))
     r_w2, r_sl, r_w1a, r_w1b, r_fr, r_sr, r_fl = [
-        Reduced(place, grad, lead, *bufs[3 * at : 3 * at + 3], dp_sems, credit, at)
+        Reduced(place, grad, lead, *bufs[4 * at : 4 * at + 4], dp_sems, credit, at)
         for at, (grad, lead) in enumerate(grads)
     ]
 
@@ -439,12 +465,13 @@
     spread_grad.start_near(2, 2)
     for copy in w_copies:
         copy.start()
-    sums_a.step_sum()
+    sums_a.step_across()
     spread_tok.wait_direct()
     turn_tokens(1)
+    sums_a.step_sum()
     turn_tokens(4)
+    turn_tokens(2)
     sums_a.step_back()
-    turn_tokens(2)
     spread_grad.pass_on(0)
     spread_tok.wait_onward()
     turn_tokens(3)
@@ -489,20 +516,20 @@
         level = at + lax.div(at, 3)
         for e in range(2):
             flow = grads_all[level, :, e * width : e * width + width]
-            g_w2[e, level] = nn(hidden_t[index_smem[level, 0, e]], flow).astype(BF)
+            g_w2[e, level] = nn(hidden_t[index_smem[level, 4 + e, level]], flow).astype(BF)
 
     repeat(4, second_grads)
     spread_grad.wait_onward()
     for e in range(2):
         flow = grads_all[3, :, e * width : e * width + width]
-        g_w2[e, 3] = nn(hidden_t[index_smem[3, 0, e]], flow).astype(BF)
+        g_w2[e, 3] = nn(hidden_t[index_smem[3, 4 + e, 3]], flow).astype(BF)
     r_w2.start(0)
 
     def hidden_back(d):
         total = nt(ranks_a[1], second_left[at_ds(d, width), :])
         for level in range(5):
             weights = [w2_all[level, e] for e in range(2)]
-            tiles = [tile_of(index_all[level, 0:1, e : e + 1], d) for e in range(2)]
+            tiles = [tile_of(index_all[level, 4 + e : 5 + e, level : level + 1], d) for e in range(2)]
             total = total + nt(grads_all[level], masked(weights, tiles))
         pre_grad[:, at_ds(d, width)] = (total * slope[d]).astype(BF)
 
@@ -542,22 +569,22 @@
     r_w2.turn(1)
 
     def out_part(level, e):
-        return nn(hidden[index_smem[level, 0, e]], w2_all[level, e])
+        return nn(hidden[index_smem[level, 4 + e, level]], w2_all[level, e])
 
     def tok_part(level, d):
         weights = [w1[f, level] for f in range(4)]
-        tiles = [tile_of(index1_rows[level, 0:1, pl.ds(f, 1)], d) for f in range(4)]
+        tiles = [tile_of(table[f : f + 1, level : level + 1], d) for f in range(4)]
         return nt(pre_grad[...], masked(weights, tiles))
 
     parts = (out_part, tok_part)
 
     def box(side, slot, block):
-        return tokens_all.at[slot, block] if side else out_in.at[slot, block]
+        return tokens_all.at[slot, block] if side else out_in.at[slot - 1, block]
 
     def remote_part(side, level, peer):
         return remote(
-            sent.at[level],
-            tokens_all.at[level] if side else out_in.at[level],
+            sent.at[level - 1],
+            tokens_all.at[level] if side else out_in.at[level - 1],
             (x_send, x_recv),
             (side, level),
             peer,
@@ -575,7 +602,7 @@
                 copies[0][level].wait_send()
 
             def step(block, level=level):
-                sent[level, block] = parts[side](level, block).astype(BF)
+                sent[level - 1, block] = parts[side](level, block).astype(BF)
 
             repeat(2, step)
             copies[side][level].start()
@@ -587,7 +614,7 @@
 
         def step(block):
             joined = parts[side](2, block) + box(side, 3, block)[...].astype(F32)
-            sent[2, block] = joined.astype(BF)
+            sent[1, block] = joined.astype(BF)
 
         repeat(2, step)
         copies[side][2].start()
@@ -606,9 +633,12 @@
 
     send_parts(0)
     r_w1a.turn(0)
-    sums_b.step_sum()
+    sums_b.step_across()
+    r_sl.relay()
+    r_w2.relay()
     send_joined(0)
     pl.semaphore_wait(inbox_free, 4)
+    r_w1b.turn(0)
     r_sl.turn(2)
     r_w2.wait(2)
     quarter = r_w2.kept[2]
@@ -625,17 +655,19 @@
     ]
     for copy in swaps:
         copy.start()
+    sums_b.step_sum()
     send_parts(1)
-    r_w1b.turn(0)
-    sums_b.step_back()
     r_w1a.turn(1)
     r_fr.turn(0)
+    sums_b.step_back()
     for copy in swaps:
         copy.wait()
     for h in range(2):
         for level in range(1, 5):
             g_w2[h, level, quarter[h], :] = swap[h, level - 1]
     r_w2.start(3)
+    r_w1b.turn(1)
+    r_w1a.relay()
     sums_b.finish()
     rank_second_t = ranks_b[0].T
     for h in range(2):
@@ -643,12 +675,13 @@
         g_fl[h, 0] = nn(tokens_t[0, h], ranks_b[1]).astype(BF)
     r_sr.start(0)
     r_fl.start(0)
-    r_w1b.turn(1)
+    r_fr.turn(1)
     r_sl.turn(3)
+    r_w1b.relay()
     send_joined(1)
-    r_fr.turn(1)
     r_w1a.turn(2)
     r_w2.turn(3)
+    r_fr.relay()
     r_sr.turn(0)
     r_fl.turn(0)
     join(0, lambda e: nn(ranks_b[0], second_right[:, at_ds(e, width)]), output)
@@ -657,6 +690,8 @@
     r_fl.turn(1)
     r_fr.turn(2)
     r_w1a.turn(3)
+    r_sr.relay()
+    r_fl.relay()
     join(1, lambda d: nt(ranks_b[1], first_left[at_ds(d, width), :]), tokens_grad)
     r_sr.turn(2)
     r_fl.turn(2)
@@ -702,9 +737,8 @@
 
     half = rank // 2
 
-    def rows_of(index):
-        wide = 128 - index.shape[0]
-        return jnp.pad(index.T[:, None, :], ((0, 0), (0, 7), (0, wide)))
+    table = jnp.concatenate([first_index, second_index], axis=0)
+    table = jnp.pad(table, ((0, 8 - table.shape[0]), (0, 128 - table.shape[1])))
 
     grads = [
         (2, 5, width, width),
@@ -717,7 +751,7 @@
     pieces = grads[:2] + [(2, 5, width, width)] * 2 + grads[3:]
     inboxes = []
     for two, count, tall, wide in pieces:
-        for step in (2, 4, 4):
+        for step in (2, 4, 4, 4):
             inboxes.append(pltpu.VMEM((two, count, tall // step, wide), BF))
     scratch = [
         pltpu.VMEM((5, features // width, rows, width), BF),
@@ -734,20 +768,22 @@
         pltpu.VMEM((2, rows, half), F32),
         pltpu.VMEM((2, rows, half), BF),
         pltpu.VMEM((2, rows, half), BF),
+        pltpu.VMEM((2, rows // 4, half), BF),
     ]
     for _ in range(2):
         scratch += [
             pltpu.VMEM((2, rows, half), BF),
-            pltpu.VMEM((7, 2, rows // 8, half), BF),
+            pltpu.VMEM((3, 2, rows // 4, half), BF),
+            pltpu.VMEM((2, rows // 4, half), BF),
             pltpu.VMEM((2, rows, rank), BF),
         ]
     scratch += [
         pltpu.VMEM((2, 4, width // 4, width), BF),
-        pltpu.VMEM((5, features // width, rows, width), BF),
-        pltpu.VMEM((5, features // width, rows, width), BF),
+        pltpu.VMEM((4, features // width, rows, width), BF),
+        pltpu.VMEM((4, features // width, rows, width), BF),
     ]
     semaphores = [dma((2 + 2 * CHUNKS,))] * 4 + [dma((16,))] * 4 + [dma((4,))] * 4
-    semaphores += [dma((7, 2, 5))] * 2 + [pltpu.SemaphoreType.REGULAR((7,))]
+    semaphores += [dma((7, 2, 6))] * 2 + [pltpu.SemaphoreType.REGULAR((7,))]
     semaphores += [dma((2, 4))] * 2 + [dma((2, 5))] * 2
     semaphores += [pltpu.SemaphoreType.REGULAR, dma((5,))]
     order = (2, 5, 3, 0, 1, 4)
@@ -755,7 +791,7 @@
         layer_kernel,
         out_shape=[shape(rows, features), shape(rows, features)]
         + [shape(*grads[at]) for at in order],
-        in_specs=[anywhere, anywhere, vmem, smem, vmem, anywhere, anywhere] + [vmem] * 4,
+        in_specs=[anywhere, anywhere, vmem, smem, anywhere, vmem] + [vmem] * 4,
         out_specs=[vmem] * 8,
         scratch_shapes=scratch + inboxes + semaphores,
         compiler_params=pltpu.CompilerParams(
@@ -767,9 +803,8 @@
         out_grad,
         first_blocks,
         first_index,
-        rows_of(first_index),
         second_blocks,
-        rows_of(second_index),
+        table,
         first_left,
         first_right,
         second_left,
@@ -787,7 +822,7 @@
         grid=(steps,),
         in_specs=specs,
         out_specs=specs,
-        compiler_params=pltpu.CompilerParams(vmem_limit_bytes=32 * 2**20),
+        compiler_params=pltpu.CompilerParams(vmem_limit_bytes=63 * 2**20),
         name="copy_kernel",
     )(*flat)
     return (

time: 255 us -> 246 us (0.965)
  local copies, waits for them, and re-layouts: 12.6 us -> 0.6 us
    unnamed x16 -> x0, local copies, waits for them, and re-layouts: 9.84 us -> none
    pallas_call x1, Pallas kernels: 3.58 us -> 7.13 us  [body(): pl.pallas_call(copy_kernel, out_shape=[shape(*result.shape) for result in...]
where the time goes in v3:
time: 246 us
  Pallas kernels  243 us (99%)
    pallas_call x1, Pallas kernels, body(): pl.pallas_call(layer_kernel, out_shape=[shape(rows, features), shape(rows...  236 us
    pallas_call x1, Pallas kernels, body(): pl.pallas_call(copy_kernel, out_shape=[shape(*result.shape) for result in...  7.13 us

profile of v3, /device:TPU:0, one launch (start us, length us, event | category | flops | bytes accessed | tf_op | source)
XLA Modules:
  0.0 245.6 jit_solution(18085324439277429073)
XLA Ops:
  0.6 0.7 pad_add_fusion
  1.3 0.6 pad.4.table
  1.9 236.3 %layer_kernel.1 = (bf16[768,512]{1,0:T(8,128)(2,1)}, bf16[768,512]{1,0:T(8,128)(2,1)}, bf16[2,10,256,256]{3,2,1,0:T(8,128)(2,1)}, bf16[2,1,256,512]{3,2,1,0:T(8,...) custom-call(bf16[768,512]{1,0:T(8,128)(2,1)} %tokens.1, ...), custom_call_target="tpu_custom_call" | custom-call | tf_op jit(solution)/shard_map/layer_kernel/pallas_call | solution.py:790
  238.3 7.1 %copy_kernel.1 = (bf16[768,512]{1,0:T(8,128)(2,1)}, bf16[768,512]{1,0:T(8,128)(2,1)}, bf16[5120,256]{1,0:T(8,128)(2,1)}, bf16[512,512]{1,0:T(8,128)(2,1)}, bf16[...) custom-call(bf16[768,512]{1,0:T(8,128)(2,1)} %get-tuple-element.24.refs_, ...), custom_call_target="tpu_custom_call" | custom-call | tf_op jit(solution)/shard_map/copy_kernel/pallas_call | solution.py:819

commit v4 on v3

--- a/solution.py
+++ b/solution.py
@@ -208,9 +208,8 @@
         self.near(chunk).wait_recv()
         self.onward(chunk).start()
 
-    def wait_direct(self):
-        for copy in self.direct:
-            copy.wait_recv()
+    def wait_slot(self, level):
+        self.direct[0 if level == 4 else 1].wait_recv()
 
     def wait_onward(self):
         repeat(CHUNKS, lambda chunk: self.onward(chunk).wait_recv())
@@ -458,31 +457,32 @@
     spread_tok.pass_on(0)
     sums_a.step_chip()
     spread_tok.pass_on(1)
+    spread_tok.wait_slot(1)
+    turn_tokens(1)
     spread_tok.pass_on(2)
-    spread_grad.start_near(0, 2)
+    spread_tok.pass_on(3)
+    sums_a.step_across()
+    spread_grad.start_near(0, 1)
+    sums_a.step_sum()
+    spread_grad.start_near(1, CHUNKS - 1)
     spread_grad.start_direct()
-    spread_tok.pass_on(3)
-    spread_grad.start_near(2, 2)
     for copy in w_copies:
         copy.start()
-    sums_a.step_across()
-    spread_tok.wait_direct()
-    turn_tokens(1)
-    sums_a.step_sum()
+    spread_tok.wait_slot(4)
     turn_tokens(4)
-    turn_tokens(2)
+    spread_tok.wait_onward()
+
+    def block_part(f):
+        picks = [tokens_all[level, index1[f, level]] for level in range(5)]
+        slope[f] = nn(jnp.concatenate(picks, axis=1), w1[f].reshape(5 * width, width))
+
+    repeat(4, block_part)
     sums_a.step_back()
     spread_grad.pass_on(0)
-    spread_tok.wait_onward()
-    turn_tokens(3)
     sums_a.finish()
-    rank_first_t[...] = ranks_a[0].T
 
     def forward(f):
-        columns = at_ds(f, width)
-        picks = [tokens_all[level, index1[f, level]] for level in range(5)]
-        pre = nn(jnp.concatenate(picks, axis=1), w1[f].reshape(5 * width, width))
-        pre = pre + nn(ranks_a[0], first_right[:, columns])
+        pre = slope[f] + nn(ranks_a[0], first_right[:, at_ds(f, width)])
         sigma = 1.0 / (1.0 + jnp.exp(-pre))
         active = (pre * sigma).astype(BF)
         hidden[f] = active
@@ -499,12 +499,11 @@
     for peer in (place.level(1), place.level(2), place.mp_peer(3), place.level(4)):
         pl.semaphore_signal(inbox_free, inc=1, device_id=peer, device_id_type=pl.DeviceIdType.MESH)
 
-    for copy in i_copies + w_copies:
+    for copy in i_copies:
         copy.wait()
     fetch = pltpu.make_async_copy(index_all, index_smem, local.at[0])
     fetch.start()
     fetch.wait()
-    spread_grad.wait_direct()
 
     def second_left_part(d):
         g_sl[lax.div(d, 2), 0, at_ds(lax.rem(d, 2), width), :] = nn(hidden_t[d], ranks_a[1]).astype(BF)
@@ -518,6 +517,12 @@
             flow = grads_all[level, :, e * width : e * width + width]
             g_w2[e, level] = nn(hidden_t[index_smem[level, 4 + e, level]], flow).astype(BF)
 
+    turn_tokens(2)
+    turn_tokens(3)
+    units = jnp.concatenate([hidden[d] for d in range(4)], axis=1)
+    sums_b.set(0, nn(units, second_left[:, mine]), nn(units, second_left[:, other]))
+    spread_grad.wait_slot(1)
+    spread_grad.wait_slot(4)
     repeat(4, second_grads)
     spread_grad.wait_onward()
     for e in range(2):
@@ -533,13 +538,14 @@
             total = total + nt(grads_all[level], masked(weights, tiles))
         pre_grad[:, at_ds(d, width)] = (total * slope[d]).astype(BF)
 
+    rank_first_t[...] = ranks_a[0].T
+    for copy in w_copies:
+        copy.wait()
     repeat(4, hidden_back)
     spread_grad.close()
     r_sl.turn(0)
     r_w2.turn(0)
 
-    units = jnp.concatenate([hidden[d] for d in range(4)], axis=1)
-    sums_b.set(0, nn(units, second_left[:, mine]), nn(units, second_left[:, other]))
     sums_b.set(1, nt(pre_grad[...], first_right[mine, :]), nt(pre_grad[...], first_right[other, :]))
     sums_b.start()
 

time: 246 us -> 231 us (0.939)
  Pallas kernels: 243 us -> 228 us
    pallas_call x1, Pallas kernels: 236 us -> 221 us  [body(): pl.pallas_call(layer_kernel, out_shape=[shape(rows, features), shape(rows...]
where the time goes in v4:
time: 231 us; the launch traced here: 230 us
  Pallas kernels  228 us (99%)
    pallas_call x1, Pallas kernels, body(): pl.pallas_call(layer_kernel, out_shape=[shape(rows, features), shape(rows...  221 us
    pallas_call x1, Pallas kernels, body(): pl.pallas_call(copy_kernel, out_shape=[shape(*result.shape) for result in...  7.13 us

profile of v4, /device:TPU:0, one launch (start us, length us, event | category | flops | bytes accessed | tf_op | source)
XLA Modules:
  0.0 229.9 jit_solution(5071214124363500798)
XLA Ops:
  0.6 0.7 pad_add_fusion
  1.3 0.6 pad.4.table
  1.9 220.6 %layer_kernel.1 = (bf16[768,512]{1,0:T(8,128)(2,1)}, bf16[768,512]{1,0:T(8,128)(2,1)}, bf16[2,10,256,256]{3,2,1,0:T(8,128)(2,1)}, bf16[2,1,256,512]{3,2,1,0:T(8,...) custom-call(bf16[768,512]{1,0:T(8,128)(2,1)} %tokens.1, ...), custom_call_target="tpu_custom_call" | custom-call | tf_op jit(solution)/shard_map/layer_kernel/pallas_call | solution.py:796
  222.6 7.1 %copy_kernel.1 = (bf16[768,512]{1,0:T(8,128)(2,1)}, bf16[768,512]{1,0:T(8,128)(2,1)}, bf16[5120,256]{1,0:T(8,128)(2,1)}, bf16[512,512]{1,0:T(8,128)(2,1)}, bf16[...) custom-call(bf16[768,512]{1,0:T(8,128)(2,1)} %get-tuple-element.24.refs_, ...), custom_call_target="tpu_custom_call" | custom-call | tf_op jit(solution)/shard_map/copy_kernel/pallas_call | solution.py:825

commit v5 on v4

--- a/solution.py
+++ b/solution.py
@@ -495,9 +495,67 @@
 
     repeat(3, forward_and_pass)
     forward(jnp.int32(3))
-    spread_tok.close()
-    for peer in (place.level(1), place.level(2), place.mp_peer(3), place.level(4)):
-        pl.semaphore_signal(inbox_free, inc=1, device_id=peer, device_id_type=pl.DeviceIdType.MESH)
+    def out_part(level, e):
+        return nn(hidden[index_smem[level, 4 + e, level]], w2_all[level, e])
+
+    def tok_part(level, d):
+        weights = [w1[f, level] for f in range(4)]
+        tiles = [tile_of(table[f : f + 1, level : level + 1], d) for f in range(4)]
+        return nt(pre_grad[...], masked(weights, tiles))
+
+    parts = (out_part, tok_part)
+
+    def box(side, slot, block):
+        return tokens_all.at[slot, block] if side else out_in.at[slot - 1, block]
+
+    def remote_part(side, level, peer):
+        return remote(
+            sent.at[level - 1],
+            tokens_all.at[level] if side else out_in.at[level - 1],
+            (x_send, x_recv),
+            (side, level),
+            peer,
+        )
+
+    peers = {1: place.level(1), 2: place.level(2), 3: place.mp_peer(3), 4: place.level(4)}
+    copies = [
+        {level: remote_part(side, level, peer) for level, peer in peers.items()}
+        for side in range(2)
+    ]
+
+    def send_part(side, level):
+        if side:
+            copies[0][level].wait_send()
+
+        def step(block):
+            sent[level - 1, block] = parts[side](level, block).astype(BF)
+
+        repeat(2, step)
+        copies[side][level].start()
+
+    def send_joined(side):
+        copies[side][3].wait_recv()
+        if side:
+            copies[0][2].wait_send()
+
+        def step(block):
+            joined = parts[side](2, block) + box(side, 3, block)[...].astype(F32)
+            sent[1, block] = joined.astype(BF)
+
+        repeat(2, step)
+        copies[side][2].start()
+
+    def join(side, rank_part, result):
+        for level in (1, 4, 2):
+            copies[side][level].wait_recv()
+
+        def step(block):
+            total = parts[side](0, block) + rank_part(block)
+            for level in (1, 4, 2):
+                total = total + box(side, level, block)[...].astype(F32)
+            result[:, at_ds(block, width)] = total.astype(BF)
+
+        repeat(2, step)
 
     for copy in i_copies:
         copy.wait()
@@ -519,6 +577,9 @@
 
     turn_tokens(2)
     turn_tokens(3)
+    spread_tok.close()
+    for peer in peers.values():
+        pl.semaphore_signal(inbox_free, inc=1, device_id=peer, device_id_type=pl.DeviceIdType.MESH)
     units = jnp.concatenate([hidden[d] for d in range(4)], axis=1)
     sums_b.set(0, nn(units, second_left[:, mine]), nn(units, second_left[:, other]))
     spread_grad.wait_slot(1)
@@ -538,9 +599,11 @@
             total = total + nt(grads_all[level], masked(weights, tiles))
         pre_grad[:, at_ds(d, width)] = (total * slope[d]).astype(BF)
 
-    rank_first_t[...] = ranks_a[0].T
     for copy in w_copies:
         copy.wait()
+    for level in (3, 4, 1):
+        send_part(0, level)
+    rank_first_t[...] = ranks_a[0].T
     repeat(4, hidden_back)
     spread_grad.close()
     r_sl.turn(0)
@@ -574,77 +637,16 @@
     r_sl.turn(1)
     r_w2.turn(1)
 
-    def out_part(level, e):
-        return nn(hidden[index_smem[level, 4 + e, level]], w2_all[level, e])
-
-    def tok_part(level, d):
-        weights = [w1[f, level] for f in range(4)]
-        tiles = [tile_of(table[f : f + 1, level : level + 1], d) for f in range(4)]
-        return nt(pre_grad[...], masked(weights, tiles))
-
-    parts = (out_part, tok_part)
-
-    def box(side, slot, block):
-        return tokens_all.at[slot, block] if side else out_in.at[slot - 1, block]
-
-    def remote_part(side, level, peer):
-        return remote(
-            sent.at[level - 1],
-            tokens_all.at[level] if side else out_in.at[level - 1],
-            (x_send, x_recv),
-            (side, level),
-            peer,
-        )
-
-    peers = {1: place.level(1), 2: place.level(2), 3: place.mp_peer(3), 4: place.level(4)}
-    copies = [
-        {level: remote_part(side, level, peer) for level, peer in peers.items()}
-        for side in range(2)
-    ]
-
-    def send_parts(side):
-        for level in (3, 4, 1):
-            if side:
-                copies[0][level].wait_send()
-
-            def step(block, level=level):
-                sent[level - 1, block] = parts[side](level, block).astype(BF)
-
-            repeat(2, step)
-            copies[side][level].start()
-
-    def send_joined(side):
-        copies[side][3].wait_recv()
-        if side:
-            copies[0][2].wait_send()
-
-        def step(block):
-            joined = parts[side](2, block) + box(side, 3, block)[...].astype(F32)
-            sent[1, block] = joined.astype(BF)
-
-        repeat(2, step)
-        copies[side][2].start()
-
-    def join(side, rank_part, result):
-        for level in (1, 4, 2):
-            copies[side][level].wait_recv()
-
-        def step(block):
-            total = parts[side](0, block) + rank_part(block)
-            for level in (1, 4, 2):
-                total = total + box(side, level, block)[...].astype(F32)
-            result[:, at_ds(block, width)] = total.astype(BF)
-
-        repeat(2, step)
-
-    send_parts(0)
+    send_joined(0)
+    sums_b.step_across()
     r_w1a.turn(0)
-    sums_b.step_across()
+    pl.semaphore_wait(inbox_free, 4)
+    send_part(1, 3)
     r_sl.relay()
     r_w2.relay()
-    send_joined(0)
-    pl.semaphore_wait(inbox_free, 4)
+    sums_b.step_sum()
     r_w1b.turn(0)
+    send_part(1, 4)
     r_sl.turn(2)
     r_w2.wait(2)
     quarter = r_w2.kept[2]
@@ -661,10 +663,8 @@
     ]
     for copy in swaps:
         copy.start()
-    sums_b.step_sum()
-    send_parts(1)
+    r_fr.turn(0)
     r_w1a.turn(1)
-    r_fr.turn(0)
     sums_b.step_back()
     for copy in swaps:
         copy.wait()
@@ -672,8 +672,6 @@
         for level in range(1, 5):
             g_w2[h, level, quarter[h], :] = swap[h, level - 1]
     r_w2.start(3)
-    r_w1b.turn(1)
-    r_w1a.relay()
     sums_b.finish()
     rank_second_t = ranks_b[0].T
     for h in range(2):
@@ -681,30 +679,33 @@
         g_fl[h, 0] = nn(tokens_t[0, h], ranks_b[1]).astype(BF)
     r_sr.start(0)
     r_fl.start(0)
+    r_w1a.relay()
+    r_w1b.turn(1)
+    r_sl.turn(3)
     r_fr.turn(1)
-    r_sl.turn(3)
     r_w1b.relay()
-    send_joined(1)
     r_w1a.turn(2)
+    r_sr.turn(0)
+    r_fl.turn(0)
     r_w2.turn(3)
     r_fr.relay()
-    r_sr.turn(0)
-    r_fl.turn(0)
-    join(0, lambda e: nn(ranks_b[0], second_right[:, at_ds(e, width)]), output)
     r_w1b.turn(2)
     r_sr.turn(1)
     r_fl.turn(1)
     r_fr.turn(2)
     r_w1a.turn(3)
+    send_part(1, 1)
     r_sr.relay()
     r_fl.relay()
-    join(1, lambda d: nt(ranks_b[1], first_left[at_ds(d, width), :]), tokens_grad)
+    send_joined(1)
+    r_w1b.turn(3)
     r_sr.turn(2)
     r_fl.turn(2)
-    r_w1b.turn(3)
     r_fr.turn(3)
+    join(0, lambda e: nn(ranks_b[0], second_right[:, at_ds(e, width)]), output)
     r_sr.turn(3)
     r_fl.turn(3)
+    join(1, lambda d: nt(ranks_b[1], first_left[at_ds(d, width), :]), tokens_grad)
     for grad in (r_sl, r_w2, r_w1a, r_w1b, r_fr, r_sr, r_fl):
         grad.wait(4)
     for level in range(1, 5):

time: 231 us -> 217 us (0.939)
  Pallas kernels: 228 us -> 214 us
    pallas_call x1, Pallas kernels: 221 us -> 207 us  [body(): pl.pallas_call(layer_kernel, out_shape=[shape(rows, features), shape(rows...]
where the time goes in v5:
time: 217 us; the launch traced here: 216 us
  Pallas kernels  214 us (99%)
    pallas_call x1, Pallas kernels, body(): pl.pallas_call(layer_kernel, out_shape=[shape(rows, features), shape(rows...  207 us
    pallas_call x1, Pallas kernels, body(): pl.pallas_call(copy_kernel, out_shape=[shape(*result.shape) for result in...  7.13 us

profile of v5, /device:TPU:0, one launch (start us, length us, event | category | flops | bytes accessed | tf_op | source)
XLA Modules:
  0.0 215.9 jit_solution(2881442630938915668)
XLA Ops:
  0.6 0.7 pad_add_fusion
  1.3 0.6 pad.4.table
  1.9 206.7 %layer_kernel.1 = (bf16[768,512]{1,0:T(8,128)(2,1)}, bf16[768,512]{1,0:T(8,128)(2,1)}, bf16[2,10,256,256]{3,2,1,0:T(8,128)(2,1)}, bf16[2,1,256,512]{3,2,1,0:T(8,...) custom-call(bf16[768,512]{1,0:T(8,128)(2,1)} %tokens.1, ...), custom_call_target="tpu_custom_call" | custom-call | tf_op jit(solution)/shard_map/layer_kernel/pallas_call | solution.py:797
  208.6 7.1 %copy_kernel.1 = (bf16[768,512]{1,0:T(8,128)(2,1)}, bf16[768,512]{1,0:T(8,128)(2,1)}, bf16[5120,256]{1,0:T(8,128)(2,1)}, bf16[512,512]{1,0:T(8,128)(2,1)}, bf16[...) custom-call(bf16[768,512]{1,0:T(8,128)(2,1)} %get-tuple-element.24.refs_, ...), custom_call_target="tpu_custom_call" | custom-call | tf_op jit(solution)/shard_map/copy_kernel/pallas_call | solution.py:826

commit v6 on v5

--- a/solution.py
+++ b/solution.py
@@ -580,8 +580,6 @@
     spread_tok.close()
     for peer in peers.values():
         pl.semaphore_signal(inbox_free, inc=1, device_id=peer, device_id_type=pl.DeviceIdType.MESH)
-    units = jnp.concatenate([hidden[d] for d in range(4)], axis=1)
-    sums_b.set(0, nn(units, second_left[:, mine]), nn(units, second_left[:, other]))
     spread_grad.wait_slot(1)
     spread_grad.wait_slot(4)
     repeat(4, second_grads)
@@ -591,26 +589,46 @@
         g_w2[e, 3] = nn(hidden_t[index_smem[3, 4 + e, 3]], flow).astype(BF)
     r_w2.start(0)
 
+    def flow_of(level, e):
+        return sent.at[level, e] if level < 4 else chip_sum.at[e]
+
     def hidden_back(d):
-        total = nt(ranks_a[1], second_left[at_ds(d, width), :])
-        for level in range(5):
-            weights = [w2_all[level, e] for e in range(2)]
-            tiles = [tile_of(index_all[level, 4 + e : 5 + e, level : level + 1], d) for e in range(2)]
-            total = total + nt(grads_all[level], masked(weights, tiles))
-        pre_grad[:, at_ds(d, width)] = (total * slope[d]).astype(BF)
+        own[0] = nt(ranks_a[1], second_left[at_ds(d, width), :])
+        tiles = [
+            [
+                jnp.broadcast_to(
+                    (index_all[level, 4 + e : 5 + e, level : level + 1] == d).astype(F32), (8, 128)
+                )
+                for e in range(2)
+            ]
+            for level in range(5)
+        ]
+
+        def step(at):
+            part = at_ds(at, 64)
+            for side in range(2):
+                lanes = pl.ds(side * 128, 128)
+                total = own[0, part, lanes].reshape(8, 8, 128)
+                for level in range(5):
+                    for e in range(2):
+                        flow = flow_of(level, e)[part, lanes].astype(F32).reshape(8, 8, 128)
+                        total = total + flow * tiles[level][e][None]
+                total = total.reshape(64, 128) * slope[d, part, lanes]
+                pre_grad[part, at_ds(2 * d + side, 128)] = total.astype(BF)
+
+        repeat(rows // 64, step)
 
     for copy in w_copies:
         copy.wait()
-    for level in (3, 4, 1):
-        send_part(0, level)
+    for level in range(5):
+        for e in range(2):
+            flow = nt(grads_all[level, :, e * width : e * width + width], w2_all[level, e])
+            flow_of(level, e)[...] = flow.astype(BF)
     rank_first_t[...] = ranks_a[0].T
     repeat(4, hidden_back)
     spread_grad.close()
     r_sl.turn(0)
     r_w2.turn(0)
-
-    sums_b.set(1, nt(pre_grad[...], first_right[mine, :]), nt(pre_grad[...], first_right[other, :]))
-    sums_b.start()
 
     def first_grads(part):
         def step(h):
@@ -630,23 +648,25 @@
 
     first_grads(0)
     r_w1a.start(0)
-    sums_b.step_chip()
     first_grads(1)
     r_w1b.start(0)
     r_fr.start(0)
     r_sl.turn(1)
     r_w2.turn(1)
 
-    send_joined(0)
-    sums_b.step_across()
+    units = jnp.concatenate([hidden[d] for d in range(4)], axis=1)
+    sums_b.set(0, nn(units, second_left[:, mine]), nn(units, second_left[:, other]))
+    sums_b.set(1, nt(pre_grad[...], first_right[mine, :]), nt(pre_grad[...], first_right[other, :]))
+    sums_b.start()
+    send_part(0, 3)
     r_w1a.turn(0)
-    pl.semaphore_wait(inbox_free, 4)
-    send_part(1, 3)
     r_sl.relay()
     r_w2.relay()
-    sums_b.step_sum()
+    sums_b.step_chip()
+    send_part(0, 4)
+    send_part(0, 1)
     r_w1b.turn(0)
-    send_part(1, 4)
+    sums_b.step_across()
     r_sl.turn(2)
     r_w2.wait(2)
     quarter = r_w2.kept[2]
@@ -665,13 +685,22 @@
         copy.start()
     r_fr.turn(0)
     r_w1a.turn(1)
-    sums_b.step_back()
+    sums_b.step_sum()
+    pl.semaphore_wait(inbox_free, 4)
+    send_part(1, 3)
     for copy in swaps:
         copy.wait()
     for h in range(2):
         for level in range(1, 5):
             g_w2[h, level, quarter[h], :] = swap[h, level - 1]
     r_w2.start(3)
+    r_w1b.turn(1)
+    r_w1a.relay()
+    sums_b.step_back()
+    send_joined(0)
+    r_sl.turn(3)
+    r_fr.turn(1)
+    r_w1b.relay()
     sums_b.finish()
     rank_second_t = ranks_b[0].T
     for h in range(2):
@@ -679,12 +708,8 @@
         g_fl[h, 0] = nn(tokens_t[0, h], ranks_b[1]).astype(BF)
     r_sr.start(0)
     r_fl.start(0)
-    r_w1a.relay()
-    r_w1b.turn(1)
-    r_sl.turn(3)
-    r_fr.turn(1)
-    r_w1b.relay()
     r_w1a.turn(2)
+    send_part(1, 4)
     r_sr.turn(0)
     r_fl.turn(0)
     r_w2.turn(3)

time: 217 us -> 221 us (1.018)
  Pallas kernels: 214 us -> 218 us
    pallas_call x1, Pallas kernels: 207 us -> 211 us  [body(): pl.pallas_call(layer_kernel, out_shape=[shape(rows, features), shape(rows...]
where the time goes in v6:
time: 221 us; the launch traced here: 220 us
  Pallas kernels  218 us (99%)
    pallas_call x1, Pallas kernels, body(): pl.pallas_call(layer_kernel, out_shape=[shape(rows, features), shape(rows...  211 us
    pallas_call x1, Pallas kernels, body(): pl.pallas_call(copy_kernel, out_shape=[shape(*result.shape) for result in...  7.13 us

profile of v6, /device:TPU:0, one launch (start us, length us, event | category | flops | bytes accessed | tf_op | source)
XLA Modules:
  0.0 220.2 jit_solution(1653024376384016507)
XLA Ops:
  0.6 0.7 pad_add_fusion
  1.3 0.6 pad.4.table
  1.9 211.0 %layer_kernel.1 = (bf16[768,512]{1,0:T(8,128)(2,1)}, bf16[768,512]{1,0:T(8,128)(2,1)}, bf16[2,10,256,256]{3,2,1,0:T(8,128)(2,1)}, bf16[2,1,256,512]{3,2,1,0:T(8,...) custom-call(bf16[768,512]{1,0:T(8,128)(2,1)} %tokens.1, ...), custom_call_target="tpu_custom_call" | custom-call | tf_op jit(solution)/shard_map/layer_kernel/pallas_call | solution.py:822
  212.9 7.1 %copy_kernel.1 = (bf16[768,512]{1,0:T(8,128)(2,1)}, bf16[768,512]{1,0:T(8,128)(2,1)}, bf16[5120,256]{1,0:T(8,128)(2,1)}, bf16[512,512]{1,0:T(8,128)(2,1)}, bf16[...) custom-call(bf16[768,512]{1,0:T(8,128)(2,1)} %get-tuple-element.24.refs_, ...), custom_call_target="tpu_custom_call" | custom-call | tf_op jit(solution)/shard_map/copy_kernel/pallas_call | solution.py:851

commit v7 on v6

--- a/solution.py
+++ b/solution.py
@@ -630,6 +630,13 @@
     r_sl.turn(0)
     r_w2.turn(0)
 
+    for level in (3, 4, 1):
+        send_part(0, level)
+    units = jnp.concatenate([hidden[d] for d in range(4)], axis=1)
+    sums_b.set(0, nn(units, second_left[:, mine]), nn(units, second_left[:, other]))
+    sums_b.set(1, nt(pre_grad[...], first_right[mine, :]), nt(pre_grad[...], first_right[other, :]))
+    sums_b.start()
+
     def first_grads(part):
         def step(h):
             f = 2 * h + part
@@ -648,25 +655,23 @@
 
     first_grads(0)
     r_w1a.start(0)
+    sums_b.step_chip()
     first_grads(1)
     r_w1b.start(0)
     r_fr.start(0)
     r_sl.turn(1)
     r_w2.turn(1)
 
-    units = jnp.concatenate([hidden[d] for d in range(4)], axis=1)
-    sums_b.set(0, nn(units, second_left[:, mine]), nn(units, second_left[:, other]))
-    sums_b.set(1, nt(pre_grad[...], first_right[mine, :]), nt(pre_grad[...], first_right[other, :]))
-    sums_b.start()
-    send_part(0, 3)
+    send_joined(0)
+    sums_b.step_across()
     r_w1a.turn(0)
+    pl.semaphore_wait(inbox_free, 4)
+    send_part(1, 3)
     r_sl.relay()
     r_w2.relay()
-    sums_b.step_chip()
-    send_part(0, 4)
-    send_part(0, 1)
+    sums_b.step_sum()
     r_w1b.turn(0)
-    sums_b.step_across()
+    send_part(1, 4)
     r_sl.turn(2)
     r_w2.wait(2)
     quarter = r_w2.kept[2]
@@ -685,22 +690,13 @@
         copy.start()
     r_fr.turn(0)
     r_w1a.turn(1)
-    sums_b.step_sum()
-    pl.semaphore_wait(inbox_free, 4)
-    send_part(1, 3)
+    sums_b.step_back()
     for copy in swaps:
         copy.wait()
     for h in range(2):
         for level in range(1, 5):
             g_w2[h, level, quarter[h], :] = swap[h, level - 1]
     r_w2.start(3)
-    r_w1b.turn(1)
-    r_w1a.relay()
-    sums_b.step_back()
-    send_joined(0)
-    r_sl.turn(3)
-    r_fr.turn(1)
-    r_w1b.relay()
     sums_b.finish()
     rank_second_t = ranks_b[0].T
     for h in range(2):
@@ -708,8 +704,12 @@
         g_fl[h, 0] = nn(tokens_t[0, h], ranks_b[1]).astype(BF)
     r_sr.start(0)
     r_fl.start(0)
+    r_w1a.relay()
+    r_w1b.turn(1)
+    r_sl.turn(3)
+    r_fr.turn(1)
+    r_w1b.relay()
     r_w1a.turn(2)
-    send_part(1, 4)
     r_sr.turn(0)
     r_fl.turn(0)
     r_w2.turn(3)

time: 221 us -> 227 us (1.027)
  Pallas kernels: 218 us -> 224 us
    pallas_call x1, Pallas kernels: 211 us -> 217 us  [body(): pl.pallas_call(layer_kernel, out_shape=[shape(rows, features), shape(rows...]
where the time goes in v7:
time: 227 us
  Pallas kernels  224 us (99%)
    pallas_call x1, Pallas kernels, body(): pl.pallas_call(layer_kernel, out_shape=[shape(rows, features), shape(rows...  217 us
    pallas_call x1, Pallas kernels, body(): pl.pallas_call(copy_kernel, out_shape=[shape(*result.shape) for result in...  7.13 us

profile of v7, /device:TPU:0, one launch (start us, length us, event | category | flops | bytes accessed | tf_op | source)
XLA Modules:
  0.0 226.6 jit_solution(10680849796898237610)
XLA Ops:
  0.6 0.7 pad_add_fusion
  1.3 0.6 pad.4.table
  1.9 217.3 %layer_kernel.1 = (bf16[768,512]{1,0:T(8,128)(2,1)}, bf16[768,512]{1,0:T(8,128)(2,1)}, bf16[2,10,256,256]{3,2,1,0:T(8,128)(2,1)}, bf16[2,1,256,512]{3,2,1,0:T(8,...) custom-call(bf16[768,512]{1,0:T(8,128)(2,1)} %tokens.1, ...), custom_call_target="tpu_custom_call" | custom-call | tf_op jit(solution)/shard_map/layer_kernel/pallas_call | solution.py:822
  219.3 7.1 %copy_kernel.1 = (bf16[768,512]{1,0:T(8,128)(2,1)}, bf16[768,512]{1,0:T(8,128)(2,1)}, bf16[5120,256]{1,0:T(8,128)(2,1)}, bf16[512,512]{1,0:T(8,128)(2,1)}, bf16[...) custom-call(bf16[768,512]{1,0:T(8,128)(2,1)} %get-tuple-element.24.refs_, ...), custom_call_target="tpu_custom_call" | custom-call | tf_op jit(solution)/shard_map/copy_kernel/pallas_call | solution.py:851
